TPU v7x, 32 devices: a whole 2x2x4 slice. The times are simulated.
32 devices in a mesh: groups: 2 (over x), gx: 4 (over y, core), gy: 4 (over z).
Axes of the slice: x: 2, y: 2, z: 4, core: 2. Of those that a mesh axis runs over, the one named last changes fastest.
Arguments:
- field_input: bfloat16 [64, 256, 1024], P(('groups', 'gx'), 'gy'), parts along dimension 0, may hold values from -8 to 8
- cotangent: bfloat16 [64, 256, 1024], P(('groups', 'gx'), 'gy'), parts along dimension 0, may hold values from -8 to 8
- spectral_weight: bfloat16 [256, 32768], P(('gx', 'gy')), may hold values from -0.75 to 0.75
- point_weight: bfloat16 [32, 32], replicated, may hold values from -1 to 1
- point_bias: float32 [32], replicated, may hold values from -3 to 3
Outputs:
- grad_field: bfloat16 [64, 256, 1024], P(('groups', 'gx'), 'gy'), parts along dimension 0
- grad_spectral: float32 [512, 32768], P(('groups', 'gx', 'gy')), parts along dimension 0
- grad_point: float32 [64, 32], P('groups'), parts along dimension 0
- grad_bias: float32 [64], P('groups'), parts along dimension 0
There are 2 independent parts, one for each index of `groups`. A program takes and returns all parts, laid end to end along the dimension named above; an argument that names none is the same for every part. Nothing has to cross between parts.
All inputs are finite; a program needn't handle non-finite values.
Results may differ from a plain program's by a relative error of at most 0.0052.
Values sent between devices are 32-bit elements; how exact they have to be, the bound alone decides.
A program may use at most 64 MiB of HBM per device.

v0:
```python
import functools
import math

import jax
import jax.numpy as jnp
import numpy as np
from jax import lax
from jax.experimental import pallas as pl
from jax.experimental.pallas import tpu as pltpu
from jax.sharding import PartitionSpec as P

C = 32
KX = 16
KY = 16
KZ = 16
NZ = 32
PM = 2 * KX
F32 = jnp.float32
BF16 = jnp.bfloat16
HIGH = lax.Precision.HIGHEST
MESH = pl.DeviceIdType.MESH


def modes(count, length):
    position = np.arange(count)
    return np.where(position < count // 2, position, length - count + position)


def angles(positions, wavenumbers, length):
    steps = positions[:, None] * wavenumbers[None, :] % length
    return 2.0 * math.pi / length * steps.astype(np.float64)


def tables(ngx, ngy, rows_x, rows_y, kk):
    full_x, full_y = ngx * rows_x, ngy * rows_y
    blocks = KZ // kk
    scale = 1.0 / math.sqrt(full_x * full_y * NZ)
    tz = angles(np.arange(NZ), np.arange(KZ), NZ)
    cz, sz = np.cos(tz), np.sin(tz)
    core = np.stack([np.stack([cz, -sz], 1), np.stack([sz, cz], 1)], 0)
    core = core.reshape(2 * NZ, 2, blocks, kk).transpose(0, 2, 1, 3).reshape(2 * NZ, 2 * KZ)
    to_modes = np.kron(core.astype(np.float32), np.eye(C, dtype=np.float32))
    ty = angles(np.arange(full_y), modes(KY, full_y), full_y).reshape(ngy, rows_y, KY)
    ytab = np.stack([np.cos(ty), -np.sin(ty)], 1).transpose(0, 1, 3, 2)
    ybd = np.einsum("gqjy,xw->gqjxwy", ytab, np.eye(rows_x))
    ybd = ybd.reshape(ngy, 2 * KY * rows_x, rows_x * rows_y)
    tx = angles(np.arange(full_x), modes(KX, full_x), full_x).T
    cx, sx = np.cos(tx) * scale, np.sin(tx) * scale
    xf = np.concatenate(
        [np.concatenate([cx, sx], 1), np.concatenate([-sx, cx], 1)], 0
    )
    n = PM * kk
    perm = np.zeros((n, n))
    r = np.arange(n)
    perm[r, (r % kk) * PM + r // kk] = 1.0
    eye = np.eye(C)
    over_out = np.repeat(eye, C, axis=1)
    over_in = np.tile(eye, (1, C))
    bf = lambda a: jnp.asarray(np.ascontiguousarray(a).astype(jnp.bfloat16))
    f32 = lambda a: jnp.asarray(np.ascontiguousarray(a).astype(np.float32))
    return dict(
        ybd=bf(ybd),
        gz=bf(to_modes),
        xf=f32(xf),
        perm=bf(perm),
        ei=bf(np.concatenate([over_out, over_out], 0)),
        ro=bf(np.tile(eye, (4, 1))),
        ybt=bf(ybd.transpose(0, 2, 1)),
        xs=f32(xf.T),
        hz=bf(to_modes.T),
        permt=bf(perm.T),
        eo=bf(np.concatenate([over_in, over_in], 0)),
        ri=bf(over_out.T),
    )


TABLES = ["ybd", "gz", "xf", "perm", "ei", "ro", "ybt", "xs", "hz", "permt", "eo", "ri"]
BY_GY = ("ybd", "ybt")


def dot(a, b):
    return jnp.dot(a, b, preferred_element_type=F32)


def dot32(a, b):
    return jnp.dot(a, b, preferred_element_type=F32, precision=HIGH)


def split(a):
    high = a.astype(BF16)
    return high, (a - high.astype(F32)).astype(BF16)


def kernel(ngx, ngy, rx, ry, kk, names, *refs):
    it = iter(refs)
    hbm = {name: next(it) for name in names}
    wp_ref, bias_ref = next(it), next(it)
    gf_out, gs_out, gp_out, gb_out = (next(it) for _ in range(4))
    vm = {name: next(it) for name in names}
    (ybuf, zout, recv1, send2, recv2, zs, recvs, fs, fin, gq, vexp, hexp, red, prod,
     adj, gs, acc, accb, kw, pbuf, precv, pbuf2, precv2) = (next(it) for _ in range(23))
    (in_sem, gs_sem, s1_send, s1_recv, s2_send, s2_recv, g_send, g_recv, f_send, f_recv,
     p_send, p_recv) = (next(it) for _ in range(12))

    gx, gy = lax.axis_index("gx"), lax.axis_index("gy")
    nx = ngx * rx
    half = kk * C
    width = 2 * half
    blocks = KZ // kk
    n = KX * kk
    scale = 1.0 / math.sqrt(nx * ngy * ry * NZ)

    loads = {}
    for i, name in enumerate(names):
        src = hbm[name].at[gy] if name in BY_GY else hbm[name]
        loads[name] = pltpu.make_async_copy(src, vm[name], in_sem.at[i])
        loads[name].start()

    barrier = pltpu.get_barrier_semaphore()
    for e in range(1, ngx):
        pl.semaphore_signal(barrier, inc=1, device_id={"gx": lax.rem(gx + e, ngx)}, device_id_type=MESH)
    for d in range(1, ngy):
        pl.semaphore_signal(barrier, inc=1, device_id={"gy": lax.rem(gy + d, ngy)}, device_id_type=MESH)

    def slab(ref, owner):
        rows = pl.ds(pl.multiple_of(owner // blocks * rx, rx), rx)
        if blocks == 1:
            return ref.at[rows]
        return ref.at[rows, pl.ds(pl.multiple_of(owner % blocks * width, width), width)]

    def lanes(b):
        return pl.ds(pl.multiple_of(b * 256, 256), 256)

    pending = []

    def forward(t, u):
        @pl.loop(0, 4)
        def _(b):
            value = dot(vm["ybd"][...], u[:, lanes(b)]).astype(BF16)
            ybuf[:, lanes(b)] = value
        if t == 0:
            loads["gz"].wait()
        rows = KY * rx

        @pl.loop(0, 4)
        def _(b):
            zout[t, :, lanes(b)] = dot(ybuf[:rows], vm["gz"][: NZ * C, lanes(b)]) + dot(
                ybuf[rows:], vm["gz"][NZ * C :, lanes(b)]
            )
        if t == 0:
            pl.semaphore_wait(barrier, ngx + ngy - 2)
        mine = pl.ds(pl.multiple_of(gx * rx, rx), rx)
        order = list(range(1, ngy)) + [0]
        for d in order:
            g = lax.rem(gy + d, ngy)
            for e in range(1, ngx):
                to = lax.rem(gx + e, ngx)
                copy = pltpu.make_async_remote_copy(
                    src_ref=slab(zout.at[t], to * ngy + g),
                    dst_ref=recv1.at[t, g, mine],
                    send_sem=s1_send.at[t, d, e - 1],
                    recv_sem=s1_recv.at[t, g],
                    device_id={"gx": to},
                    device_id_type=MESH,
                )
                copy.start()
                pending.append(copy)
            recv1[t, g, mine] = slab(zout.at[t], gx * ngy + g)[...]

    def gather_modes(t):
        order = list(range(1, ngy)) + [0]
        for d in order:
            g = lax.rem(gy + d, ngy)
            got = recv1.at[t, g, pl.ds(0, (ngx - 1) * rx)]
            pltpu.make_async_copy(got, got, s1_recv.at[t, g]).wait()
            value = dot32(vm["xf"][:, :nx], recv1[t, g, :, :half]) + dot32(
                vm["xf"][:, nx:], recv1[t, g, :, half:]
            )
            if d == 0:
                recv2[t, gy] = value
            else:
                send2[t, d] = value
                copy = pltpu.make_async_remote_copy(
                    src_ref=send2.at[t, d],
                    dst_ref=recv2.at[t, gy],
                    send_sem=s2_send.at[t, d],
                    recv_sem=s2_recv.at[t],
                    device_id={"gy": g},
                    device_id_type=MESH,
                )
                copy.start()
                pending.append(copy)
        got = recv2.at[t, pl.ds(0, ngy - 1)]
        pltpu.make_async_copy(got, got, s2_recv.at[t]).wait()
        total = recv2[t, 0]
        for g in range(1, ngy):
            total = total + recv2[t, g]
        return total

    def scatter_modes(t, value):
        zs[t] = value
        for d in range(1, ngy):
            copy = pltpu.make_async_remote_copy(
                src_ref=zs.at[t],
                dst_ref=recvs.at[t, gy],
                send_sem=g_send.at[t, d],
                recv_sem=g_recv.at[t, gy],
                device_id={"gy": lax.rem(gy + d, ngy)},
                device_id_type=MESH,
            )
            copy.start()
            pending.append(copy)
        mine = pl.ds(pl.multiple_of(gx * rx, rx), rx)
        for d in range(ngy):
            g = lax.rem(gy + d, ngy)
            if d == 0:
                block = value
            else:
                got = recvs.at[t, g]
                pltpu.make_async_copy(got, got, g_recv.at[t, g]).wait()
                block = recvs[t, g]
            fs[t, g, :, :half] = dot32(vm["xs"][:nx], block)
            fs[t, g, :, half:] = dot32(vm["xs"][nx:], block)
            owner = gx * ngy + g
            for e in range(1, ngx):
                to = lax.rem(gx + e, ngx)
                copy = pltpu.make_async_remote_copy(
                    src_ref=fs.at[t, g, pl.ds(pl.multiple_of(to * rx, rx), rx)],
                    dst_ref=slab(fin.at[t], owner),
                    send_sem=f_send.at[t, d, e - 1],
                    recv_sem=f_recv.at[t],
                    device_id={"gx": to},
                    device_id_type=MESH,
                )
                copy.start()
                pending.append(copy)
            slab(fin.at[t], owner)[...] = fs[t, g, mine]

    def backward(t):
        got = fin.at[t, pl.ds(0, KY * rx // ngx * (ngx - 1))]
        pltpu.make_async_copy(got, got, f_recv.at[t]).wait()
        rows = KY * rx
        ybuf[:rows] = fin[t].astype(BF16)

        @pl.loop(0, 4)
        def _(b):
            gq[:rows, lanes(b)] = dot(ybuf[:rows], vm["hz"][:, lanes(b)]).astype(BF16)

        @pl.loop(0, 4)
        def _(b):
            gq[rows:, lanes(b)] = dot(ybuf[:rows], vm["hz"][:, lanes(b + 4)]).astype(BF16)

    def to_rows(value):
        stack = jnp.concatenate([value[:, k * C : (k + 1) * C] for k in range(kk)], axis=0)
        high = stack.astype(BF16).astype(F32)
        both = jnp.concatenate([high, stack - high], axis=1).astype(BF16)
        return dot(vm["perm"][...], both).astype(BF16)

    def from_rows(value):
        high = value.astype(BF16).astype(F32)
        both = jnp.concatenate([high, value - high], axis=1).astype(BF16)
        moved = dot(vm["permt"][...], both)
        moved = moved[:, :C] + moved[:, C:]
        return jnp.concatenate([moved[k * PM : (k + 1) * PM] for k in range(kk)], axis=1)

    lane = lax.broadcasted_iota(jnp.int32, (PM, half), 1)
    first_k = (gx * ngy + gy) % blocks * kk
    doubling = jnp.where(lane // C + first_k == 0, 1.0, 2.0).astype(F32)

    row = lax.broadcasted_iota(jnp.int32, (256, C), 0) % C
    col = lax.broadcasted_iota(jnp.int32, (256, C), 1)
    sel = (row == col).astype(F32).astype(BF16)
    tall = dot(sel, wp_ref[...]).astype(BF16)
    wide = lax.dot_general(tall, sel, (((1,), (1,)), ((), ())), preferred_element_type=F32)
    br = lax.broadcasted_iota(jnp.int32, (256, 256), 0) // C
    bc = lax.broadcasted_iota(jnp.int32, (256, 256), 1) // C
    kw[...] = jnp.where(br == bc, wide, 0.0).astype(BF16)
    bias = jnp.concatenate([bias_ref[...]] * 8, axis=1)

    loads["field"].wait()
    loads["ybd"].wait()
    forward(0, vm["field"])
    for name in names:
        if name not in ("field", "ybd", "gz"):
            loads[name].wait()
    spec = gather_modes(0)

    vexp[...] = dot(to_rows(spec), vm["ei"][...])
    for m in range(KX):
        a, b = slice(m * kk, (m + 1) * kk), slice(n + m * kk, n + (m + 1) * kk)
        vr, vi = vexp[a], vexp[b]
        wr = vm["weight"][:, m * 2048 : m * 2048 + 1024].astype(F32)
        wi = vm["weight"][:, m * 2048 + 1024 : m * 2048 + 2048].astype(F32)
        pr = vr * wr - vi * wi
        pi = vr * wi + vi * wr
        red[a] = sum(pr[:, s * 128 : (s + 1) * 128] for s in range(8))
        red[b] = sum(pi[:, s * 128 : (s + 1) * 128] for s in range(8))
    high, low = split(red[...])
    out = dot(high, vm["ro"][...]) + dot(low, vm["ro"][...])
    scatter_modes(0, from_rows(out) * doubling)
    backward(0)

    @pl.loop(0, 4)
    def _(b):
        mixed = dot(vm["field"][:, lanes(b)], kw[...])
        v = dot(vm["ybt"][...], gq[:, lanes(b)]) + mixed + bias
        root = math.sqrt(2.0 / math.pi)
        square = v * v
        th = jnp.tanh(root * v * (1.0 + 0.044715 * square))
        slope = 0.5 * (1.0 + th) + 0.5 * v * (1.0 - th * th) * (
            root * (1.0 + 3 * 0.044715 * square)
        )
        adj[:, lanes(b)] = (vm["cot"][:, lanes(b)].astype(F32) * slope).astype(BF16)

    forward(1, adj)

    acc[...] = jnp.zeros_like(acc)
    accb[...] = jnp.zeros_like(accb)
    ones = jnp.ones((16, rx * ry), BF16)

    @pl.loop(0, 4)
    def _(b):
        block = adj[:, lanes(b)]
        acc[...] += lax.dot_general(
            vm["field"][:, lanes(b)], block, (((0,), (0,)), ((), ())), preferred_element_type=F32
        )
        accb[...] += dot(ones, block)

    pbuf[...] = jnp.zeros_like(pbuf)
    pbuf[:C, :C] = sum(acc[i * C : (i + 1) * C, i * C : (i + 1) * C] for i in range(8)) * scale
    pbuf[C:, :C] = sum(accb[:8, i * C : (i + 1) * C] for i in range(8)) * scale
    for e in range(1, ngx):
        copy = pltpu.make_async_remote_copy(
            src_ref=pbuf,
            dst_ref=precv.at[gx],
            send_sem=p_send.at[e],
            recv_sem=p_recv.at[0],
            device_id={"gx": lax.rem(gx + e, ngx)},
            device_id_type=MESH,
        )
        copy.start()
        pending.append(copy)
    precv[gx] = pbuf[...]

    spec = gather_modes(1) * doubling
    hexp[...] = dot(to_rows(spec), vm["eo"][...])
    for m in range(KX):
        a, b = slice(m * kk, (m + 1) * kk), slice(n + m * kk, n + (m + 1) * kk)
        hr, hi = hexp[a], hexp[b]
        wr = vm["weight"][:, m * 2048 : m * 2048 + 1024].astype(F32)
        wi = vm["weight"][:, m * 2048 + 1024 : m * 2048 + 2048].astype(F32)
        prod[a] = hr * wr + hi * wi
        prod[b] = hi * wr - hr * wi
    high, low = split(prod[...])
    out = dot(high, vm["ri"][...]) + dot(low, vm["ri"][...])
    scatter_modes(1, from_rows(out))

    got = precv.at[pl.ds(0, ngx - 1)]
    pltpu.make_async_copy(got, got, p_recv.at[0]).wait()
    pbuf2[...] = sum(precv[i] for i in range(ngx))
    for d in range(1, ngy):
        copy = pltpu.make_async_remote_copy(
            src_ref=pbuf2,
            dst_ref=precv2.at[gy],
            send_sem=p_send.at[ngx + d],
            recv_sem=p_recv.at[1],
            device_id={"gy": lax.rem(gy + d, ngy)},
            device_id_type=MESH,
        )
        copy.start()
        pending.append(copy)
    precv2[gy] = pbuf2[...]

    for m in range(KX):
        a, b = slice(m * kk, (m + 1) * kk), slice(n + m * kk, n + (m + 1) * kk)
        vr, vi, hr, hi = vexp[a], vexp[b], hexp[a] * scale, hexp[b] * scale
        gs[:, m * 2048 : m * 2048 + 1024] = vr * hr + vi * hi
        gs[:, m * 2048 + 1024 : m * 2048 + 2048] = vr * hi - vi * hr
    gs_copy = pltpu.make_async_copy(gs, gs_out, gs_sem)
    gs_copy.start()

    backward(1)

    @pl.loop(0, 4)
    def _(b):
        back = lax.dot_general(
            adj[:, lanes(b)], kw[...], (((1,), (1,)), ((), ())), preferred_element_type=F32
        )
        gf_out[:, lanes(b)] = (dot(vm["ybt"][...], gq[:, lanes(b)]) + back).astype(BF16)

    got = precv2.at[pl.ds(0, ngy - 1)]
    pltpu.make_async_copy(got, got, p_recv.at[1]).wait()
    total = sum(precv2[i] for i in range(ngy))
    gp_out[...] = total[:C, :C]
    gb_out[...] = total[C : C + 1, :C]
    gs_copy.wait()
    for copy in pending:
        copy.wait_send()


def on_device(ngx, ngy, field_input, cotangent, spectral_weight, point_weight, point_bias):
    rx, ry, depth = field_input.shape
    kk = spectral_weight.shape[0]
    cells = rx * ry
    nx = rx * ngx
    half, width = kk * C, 2 * kk * C
    arrays = dict(field=field_input.reshape(cells, depth))
    consts = tables(ngx, ngy, rx, ry, kk)
    arrays["ybd"] = consts["ybd"]
    arrays["gz"] = consts["gz"]
    arrays["xf"] = consts["xf"]
    arrays["weight"] = spectral_weight
    for name in TABLES:
        arrays[name] = consts[name]
    arrays["cot"] = cotangent.reshape(cells, depth)
    names = tuple(arrays)
    local = [
        pltpu.VMEM(a.shape[1:] if k in BY_GY else a.shape, a.dtype) for k, a in arrays.items()
    ]
    rows = KY * rx
    n2 = PM * kk
    vmem = pl.BlockSpec(memory_space=pltpu.VMEM)
    hbm = pl.BlockSpec(memory_space=pl.ANY)
    dma = pltpu.SemaphoreType.DMA
    grad_field, grad_spectral, grad_point, grad_bias = pl.pallas_call(
        functools.partial(kernel, ngx, ngy, rx, ry, kk, names),
        out_shape=(
            jax.ShapeDtypeStruct((cells, depth), BF16),
            jax.ShapeDtypeStruct(spectral_weight.shape, F32),
            jax.ShapeDtypeStruct((C, C), F32),
            jax.ShapeDtypeStruct((1, C), F32),
        ),
        in_specs=[hbm] * len(names) + [vmem, vmem],
        out_specs=(vmem, hbm, vmem, vmem),
        scratch_shapes=local
        + [
            pltpu.VMEM((2 * rows, depth), BF16),
            pltpu.VMEM((2, rows, depth), F32),
            pltpu.VMEM((2, ngy, nx, width), F32),
            pltpu.VMEM((2, ngy, PM, half), F32),
            pltpu.VMEM((2, ngy, PM, half), F32),
            pltpu.VMEM((2, PM, half), F32),
            pltpu.VMEM((2, ngy, PM, half), F32),
            pltpu.VMEM((2, ngy, nx, width), F32),
            pltpu.VMEM((2, rows, depth), F32),
            pltpu.VMEM((2 * rows, depth), BF16),
            pltpu.VMEM((n2, C * C), F32),
            pltpu.VMEM((n2, C * C), F32),
            pltpu.VMEM((n2, 128), F32),
            pltpu.VMEM((n2, C * C), F32),
            pltpu.VMEM((cells, depth), BF16),
            pltpu.VMEM(spectral_weight.shape, F32),
            pltpu.VMEM((256, 256), F32),
            pltpu.VMEM((16, 256), F32),
            pltpu.VMEM((256, 256), BF16),
            pltpu.VMEM((C + 8, 128), F32),
            pltpu.VMEM((ngx, C + 8, 128), F32),
            pltpu.VMEM((C + 8, 128), F32),
            pltpu.VMEM((ngy, C + 8, 128), F32),
            dma((len(names),)),
            dma,
            dma((2, ngy, ngx - 1)),
            dma((2, ngy)),
            dma((2, ngy)),
            dma((2,)),
            dma((2, ngy)),
            dma((2, ngy)),
            dma((2, ngy, ngx - 1)),
            dma((2,)),
            dma((ngx + ngy,)),
            dma((2,)),
        ],
        compiler_params=pltpu.CompilerParams(
            collective_id=0, has_side_effects=True, vmem_limit_bytes=52 * 1024 * 1024
        ),
    )(*arrays.values(), point_weight, point_bias.reshape(1, C))
    return (
        grad_field.reshape(rx, ry, depth),
        grad_spectral,
        grad_point,
        grad_bias.reshape(C),
    )


def solution(mesh):
    return jax.shard_map(
        functools.partial(on_device, mesh.shape["gx"], mesh.shape["gy"]),
        mesh=mesh,
        in_specs=(
            P(("groups", "gx"), "gy", None),
            P(("groups", "gx"), "gy", None),
            P(("gx", "gy"), None),
            P(),
            P(),
        ),
        out_specs=(
            P(("groups", "gx"), "gy", None),
            P(("groups", "gx", "gy"), None),
            P("groups", None),
            P("groups"),
        ),
        check_vma=False,
    )
```

profile of v0, /device:TPU:0, one launch (start us, length us, event | category | flops | bytes accessed | tf_op | source)
XLA Modules:
  0.0 86.4 jit_solution(2489937182378936644)
XLA Ops:
  0.6 0.0 copy-start
  0.6 1.0 %copy-done = bf16[512,512]{1,0:T(8,128)(2,1)S(1)} copy-done((bf16[512,512]{1,0:T(8,128)(2,1)S(1)}, bf16[512,512]{1,0:T(8,128)(2,1)}, u32[]{:S(2)}) %copy-start) | copy-done | bytes 524312
  1.7 0.0 copy-start.1
  1.7 1.0 %copy-done.1 = bf16[512,512]{1,0:T(8,128)(2,1)S(1)} copy-done((bf16[512,512]{1,0:T(8,128)(2,1)S(1)}, bf16[512,512]{1,0:T(8,128)(2,1)}, u32[]{:S(2)}) %copy-start.1) | copy-done | bytes 524312
  2.7 0.0 copy-start.2
  2.7 0.9 %copy-done.2 = bf16[1024,32]{1,0:T(8,128)(2,1)S(1)} copy-done((bf16[1024,32]{1,0:T(8,128)(2,1)S(1)}, bf16[1024,32]{1,0:T(8,128)(2,1)}, u32[]{:S(2)}) %copy-start.2) | copy-done | bytes 65560
  3.7 0.0 copy-start.3
  3.7 0.9 %copy-done.3 = bf16[64,1024]{1,0:T(8,128)(2,1)S(1)} copy-done((bf16[64,1024]{1,0:T(8,128)(2,1)S(1)}, bf16[64,1024]{1,0:T(8,128)(2,1)}, u32[]{:S(2)}) %copy-start.3) | copy-done | bytes 131096
  4.6 0.0 copy-start.4
  4.6 0.9 %copy-done.4 = bf16[64,1024]{1,0:T(8,128)(2,1)S(1)} copy-done((bf16[64,1024]{1,0:T(8,128)(2,1)S(1)}, bf16[64,1024]{1,0:T(8,128)(2,1)}, u32[]{:S(2)}) %copy-start.4) | copy-done | bytes 131096
  5.5 0.0 copy-start.5
  5.5 0.8 copy-done.5
  6.2 0.0 copy-start.6
  6.2 0.8 copy-done.6
  7.0 0.0 copy-start.7
  7.0 0.7 copy-done.7
  7.7 0.0 copy-start.8
  7.7 0.7 copy-done.8
  8.4 0.0 copy-start.9
  8.4 0.7 copy-done.9
  9.1 70.9 %shard_map.192 = (bf16[512,1024]{1,0:T(8,128)(2,1)}, f32[16,32768]{1,0:T(8,128)}, f32[32,32]{1,0:T(8,128)S(1)}, f32[1,32]{1,0:T(1,128)S(1)}) custom-call(bf16[512,1024]{1,0:T(8,128)(2,1)} %bitcast.7, bf16[4,256,512]{2,1,0:T(8,128)(2,1)} %constant.24.clone.refs_1_, bf16[2048,1024]{1,0:T(8,128)(2,1)} %constant.25.clone.refs_2_, f32[32,64]{1,0:T(8,128)S(1)} %copy-done.7, ...), custom_call_target="tpu_custom_call" | custom-call | tf_op jit(solution)/shard_map/pallas_call | solution.py:425
  80.0 2.3 %copy.25 = bf16[8,64,1024]{2,1,0:T(8,128)(2,1)} copy(bf16[8,64,1024]{2,1,0:T(8,128)(2,1)} %bitcast.9) | data formatting | bytes 2097152
  82.2 3.0 %copy.26 = f32[16,32768]{1,0:T(8,128)} copy(f32[16,32768]{1,0:T(8,128)} %get-tuple-element.17) | data formatting | bytes 4194304
  85.3 0.6 copy.27
  85.9 0.5 copy.28
Async XLA Ops:
  0.6 1.0 %copy-start = (bf16[512,512]{1,0:T(8,128)(2,1)S(1)}, bf16[512,512]{1,0:T(8,128)(2,1)}, u32[]{:S(2)}) copy-start(bf16[512,512]{1,0:T(8,128)(2,1)} %constant.33.clone.refs_11_) | copy-start | bytes 1572868
  1.7 1.0 %copy-start.1 = (bf16[512,512]{1,0:T(8,128)(2,1)S(1)}, bf16[512,512]{1,0:T(8,128)(2,1)}, u32[]{:S(2)}) copy-start(bf16[512,512]{1,0:T(8,128)(2,1)} %constant.27.clone.refs_5_) | copy-start | bytes 1572868
  2.7 0.9 %copy-start.2 = (bf16[1024,32]{1,0:T(8,128)(2,1)S(1)}, bf16[1024,32]{1,0:T(8,128)(2,1)}, u32[]{:S(2)}) copy-start(bf16[1024,32]{1,0:T(8,128)(2,1)} %constant.35.clone.refs_13_) | copy-start | bytes 196612
  3.7 0.9 %copy-start.3 = (bf16[64,1024]{1,0:T(8,128)(2,1)S(1)}, bf16[64,1024]{1,0:T(8,128)(2,1)}, u32[]{:S(2)}) copy-start(bf16[64,1024]{1,0:T(8,128)(2,1)} %constant.34.clone.refs_12_) | copy-start | bytes 393220
  4.6 0.9 %copy-start.4 = (bf16[64,1024]{1,0:T(8,128)(2,1)S(1)}, bf16[64,1024]{1,0:T(8,128)(2,1)}, u32[]{:S(2)}) copy-start(bf16[64,1024]{1,0:T(8,128)(2,1)} %constant.28.clone.refs_6_) | copy-start | bytes 393220
  5.5 0.8 copy-start.5
  6.2 0.8 copy-start.6
  7.0 0.7 copy-start.7
  7.7 0.7 copy-start.8
  8.4 0.7 copy-start.9
where the time goes:
time: 87 us; the launch traced here: 86.4 us
  Pallas kernels  70.9 us (81%)
  local copies, waits for them, and re-layouts  14.8 us (17%)
    pallas_call x1, Pallas kernels, on_device(): pl.pallas_call(functools.partial(kernel, ngx, ngy, rx, ry, kk, names), ou...  70.9 us
    unnamed x24, local copies, waits for them, and re-layouts  14.8 us

commit v1 on v0

--- a/solution.py
+++ b/solution.py
@@ -17,7 +17,6 @@
 PM = 2 * KX
 F32 = jnp.float32
 BF16 = jnp.bfloat16
-HIGH = lax.Precision.HIGHEST
 MESH = pl.DeviceIdType.MESH
 
 
@@ -33,13 +32,15 @@
 
 def tables(ngx, ngy, rows_x, rows_y, kk):
     full_x, full_y = ngx * rows_x, ngy * rows_y
-    blocks = KZ // kk
     scale = 1.0 / math.sqrt(full_x * full_y * NZ)
     tz = angles(np.arange(NZ), np.arange(KZ), NZ)
-    cz, sz = np.cos(tz), np.sin(tz)
-    core = np.stack([np.stack([cz, -sz], 1), np.stack([sz, cz], 1)], 0)
-    core = core.reshape(2 * NZ, 2, blocks, kk).transpose(0, 2, 1, 3).reshape(2 * NZ, 2 * KZ)
-    to_modes = np.kron(core.astype(np.float32), np.eye(C, dtype=np.float32))
+    eye = np.eye(C, dtype=np.float32)
+    to_modes = np.concatenate(
+        [np.kron(f(tz).astype(np.float32), eye) for f in (np.cos, np.sin)], 1
+    )
+    from_modes = np.concatenate(
+        [np.kron(f(tz).astype(np.float32).T, eye) for f in (np.cos, np.sin)], 1
+    )
     ty = angles(np.arange(full_y), modes(KY, full_y), full_y).reshape(ngy, rows_y, KY)
     ytab = np.stack([np.cos(ty), -np.sin(ty)], 1).transpose(0, 1, 3, 2)
     ybd = np.einsum("gqjy,xw->gqjxwy", ytab, np.eye(rows_x))
@@ -49,32 +50,24 @@
     xf = np.concatenate(
         [np.concatenate([cx, sx], 1), np.concatenate([-sx, cx], 1)], 0
     )
-    n = PM * kk
-    perm = np.zeros((n, n))
-    r = np.arange(n)
-    perm[r, (r % kk) * PM + r // kk] = 1.0
-    eye = np.eye(C)
-    over_out = np.repeat(eye, C, axis=1)
-    over_in = np.tile(eye, (1, C))
-    bf = lambda a: jnp.asarray(np.ascontiguousarray(a).astype(jnp.bfloat16))
-    f32 = lambda a: jnp.asarray(np.ascontiguousarray(a).astype(np.float32))
+    bf = lambda a: np.ascontiguousarray(a).astype(jnp.bfloat16)
+
+    def three(a):
+        high = bf(a)
+        low = bf(a - high.astype(np.float64))
+        return jnp.asarray(np.concatenate([high, high, low], 1))
+
     return dict(
-        ybd=bf(ybd),
-        gz=bf(to_modes),
-        xf=f32(xf),
-        perm=bf(perm),
-        ei=bf(np.concatenate([over_out, over_out], 0)),
-        ro=bf(np.tile(eye, (4, 1))),
-        ybt=bf(ybd.transpose(0, 2, 1)),
-        xs=f32(xf.T),
-        hz=bf(to_modes.T),
-        permt=bf(perm.T),
-        eo=bf(np.concatenate([over_in, over_in], 0)),
-        ri=bf(over_out.T),
+        ybd=jnp.asarray(bf(ybd)),
+        gz=jnp.asarray(bf(to_modes)),
+        xf=three(xf),
+        ybt=jnp.asarray(bf(ybd.transpose(0, 2, 1))),
+        xs=three(xf.T),
+        hz=jnp.asarray(bf(from_modes)),
     )
 
 
-TABLES = ["ybd", "gz", "xf", "perm", "ei", "ro", "ybt", "xs", "hz", "permt", "eo", "ri"]
+TABLES = ["ybd", "gz", "xf", "ybt", "xs", "hz"]
 BY_GY = ("ybd", "ybt")
 
 
@@ -82,8 +75,9 @@
     return jnp.dot(a, b, preferred_element_type=F32)
 
 
-def dot32(a, b):
-    return jnp.dot(a, b, preferred_element_type=F32, precision=HIGH)
+def dot3(table, b):
+    high, low = split(b)
+    return dot(table, jnp.concatenate([high, low, high], axis=0))
 
 
 def split(a):
@@ -94,13 +88,13 @@
 def kernel(ngx, ngy, rx, ry, kk, names, *refs):
     it = iter(refs)
     hbm = {name: next(it) for name in names}
-    wp_ref, bias_ref = next(it), next(it)
     gf_out, gs_out, gp_out, gb_out = (next(it) for _ in range(4))
     vm = {name: next(it) for name in names}
     (ybuf, zout, recv1, send2, recv2, zs, recvs, fs, fin, gq, vexp, hexp, red, prod,
-     adj, gs, acc, accb, kw, pbuf, precv, pbuf2, precv2) = (next(it) for _ in range(23))
-    (in_sem, gs_sem, s1_send, s1_recv, s2_send, s2_recv, g_send, g_recv, f_send, f_recv,
-     p_send, p_recv) = (next(it) for _ in range(12))
+     adj, gs, acc, accb, kw, pbuf, precv, pbuf2, precv2, f2, pre, gf, perm, permt, ei, eo,
+     ro, ri) = (next(it) for _ in range(32))
+    (in_sem, gs_sem, gf_sem, s1_send, s1_recv, s2_send, s2_recv, g_send, g_recv, f_send, f_recv,
+     p_send, p_recv) = (next(it) for _ in range(13))
 
     gx, gy = lax.axis_index("gx"), lax.axis_index("gy")
     nx = ngx * rx
@@ -131,34 +125,47 @@
     def lanes(b):
         return pl.ds(pl.multiple_of(b * 256, 256), 256)
 
+    chips = ngx // 2
+    chip, core = gx // 2, gx % 2
+    steps = [(c, k) for c in range(1, chips) for k in range(2)] + [(0, 1)]
+    peers = [lax.rem(chip + c, chips) * 2 + lax.rem(core + k, 2) for c, k in steps]
+    way = 1 - 2 * (gy // (ngy // 2))
+
+    def along(d):
+        return lax.rem(gy + way * d + ngy, ngy)
+
+    far_first = list(range(ngy - 1, -1, -1))
     pending = []
 
+    rows = KY * rx
+
     def forward(t, u):
-        @pl.loop(0, 4)
-        def _(b):
-            value = dot(vm["ybd"][...], u[:, lanes(b)]).astype(BF16)
-            ybuf[:, lanes(b)] = value
+        for b in range(4):
+            at = slice(b * 256, b * 256 + 256)
+            ybuf[:, at] = dot(vm["ybd"][...], u[:, at]).astype(BF16)
         if t == 0:
             loads["gz"].wait()
-        rows = KY * rx
-
-        @pl.loop(0, 4)
-        def _(b):
-            zout[t, :, lanes(b)] = dot(ybuf[:rows], vm["gz"][: NZ * C, lanes(b)]) + dot(
-                ybuf[rows:], vm["gz"][NZ * C :, lanes(b)]
-            )
+        for b in range(2):
+            cos = dot(ybuf[...], vm["gz"][:, b * 256 : b * 256 + 256])
+            sin = dot(ybuf[...], vm["gz"][:, KZ * C + b * 256 : KZ * C + b * 256 + 256])
+            real = cos[:rows] + sin[rows:]
+            imag = cos[rows:] - sin[:rows]
+            part = min(half, 256)
+            for i in range(256 // part):
+                lane0 = b * 256 + i * part
+                at = lane0 // half * width + lane0 % half
+                zout[t, :, at : at + part] = real[:, i * part : (i + 1) * part]
+                zout[t, :, at + half : at + half + part] = imag[:, i * part : (i + 1) * part]
         if t == 0:
             pl.semaphore_wait(barrier, ngx + ngy - 2)
         mine = pl.ds(pl.multiple_of(gx * rx, rx), rx)
-        order = list(range(1, ngy)) + [0]
-        for d in order:
-            g = lax.rem(gy + d, ngy)
-            for e in range(1, ngx):
-                to = lax.rem(gx + e, ngx)
+        for d in far_first:
+            g = along(d)
+            for e, to in enumerate(peers):
                 copy = pltpu.make_async_remote_copy(
                     src_ref=slab(zout.at[t], to * ngy + g),
                     dst_ref=recv1.at[t, g, mine],
-                    send_sem=s1_send.at[t, d, e - 1],
+                    send_sem=s1_send.at[t, d, e],
                     recv_sem=s1_recv.at[t, g],
                     device_id={"gx": to},
                     device_id_type=MESH,
@@ -168,14 +175,12 @@
             recv1[t, g, mine] = slab(zout.at[t], gx * ngy + g)[...]
 
     def gather_modes(t):
-        order = list(range(1, ngy)) + [0]
-        for d in order:
-            g = lax.rem(gy + d, ngy)
+        for d in far_first:
+            g = along(d)
             got = recv1.at[t, g, pl.ds(0, (ngx - 1) * rx)]
             pltpu.make_async_copy(got, got, s1_recv.at[t, g]).wait()
-            value = dot32(vm["xf"][:, :nx], recv1[t, g, :, :half]) + dot32(
-                vm["xf"][:, nx:], recv1[t, g, :, half:]
-            )
+            both = jnp.concatenate([recv1[t, g, :, :half], recv1[t, g, :, half:]], axis=0)
+            value = dot3(vm["xf"][...], both)
             if d == 0:
                 recv2[t, gy] = value
             else:
@@ -205,29 +210,29 @@
                 dst_ref=recvs.at[t, gy],
                 send_sem=g_send.at[t, d],
                 recv_sem=g_recv.at[t, gy],
-                device_id={"gy": lax.rem(gy + d, ngy)},
+                device_id={"gy": along(d)},
                 device_id_type=MESH,
             )
             copy.start()
             pending.append(copy)
         mine = pl.ds(pl.multiple_of(gx * rx, rx), rx)
         for d in range(ngy):
-            g = lax.rem(gy + d, ngy)
+            g = along(d)
             if d == 0:
                 block = value
             else:
                 got = recvs.at[t, g]
                 pltpu.make_async_copy(got, got, g_recv.at[t, g]).wait()
                 block = recvs[t, g]
-            fs[t, g, :, :half] = dot32(vm["xs"][:nx], block)
-            fs[t, g, :, half:] = dot32(vm["xs"][nx:], block)
+            both = dot3(vm["xs"][...], block)
+            fs[t, g, :, :half] = both[:nx]
+            fs[t, g, :, half:] = both[nx:]
             owner = gx * ngy + g
-            for e in range(1, ngx):
-                to = lax.rem(gx + e, ngx)
+            for e, to in enumerate(peers):
                 copy = pltpu.make_async_remote_copy(
                     src_ref=fs.at[t, g, pl.ds(pl.multiple_of(to * rx, rx), rx)],
                     dst_ref=slab(fin.at[t], owner),
-                    send_sem=f_send.at[t, d, e - 1],
+                    send_sem=f_send.at[t, d, e],
                     recv_sem=f_recv.at[t],
                     device_id={"gx": to},
                     device_id_type=MESH,
@@ -239,43 +244,33 @@
     def backward(t):
         got = fin.at[t, pl.ds(0, KY * rx // ngx * (ngx - 1))]
         pltpu.make_async_copy(got, got, f_recv.at[t]).wait()
-        rows = KY * rx
-        ybuf[:rows] = fin[t].astype(BF16)
-
-        @pl.loop(0, 4)
-        def _(b):
-            gq[:rows, lanes(b)] = dot(ybuf[:rows], vm["hz"][:, lanes(b)]).astype(BF16)
-
-        @pl.loop(0, 4)
-        def _(b):
-            gq[rows:, lanes(b)] = dot(ybuf[:rows], vm["hz"][:, lanes(b + 4)]).astype(BF16)
+        for kb in range(blocks):
+            at, to = kb * width, slice(kb * half, (kb + 1) * half)
+            f2[:rows, to] = fin[t, :, at : at + half].astype(BF16)
+            f2[rows:, to] = fin[t, :, at + half : at + width].astype(BF16)
+        for b in range(4):
+            at = slice(b * 256, b * 256 + 256)
+            cos = dot(f2[...], vm["hz"][:, at])
+            sin = dot(f2[...], vm["hz"][:, NZ * C + b * 256 : NZ * C + b * 256 + 256])
+            gq[:rows, at] = (cos[:rows] - sin[rows:]).astype(BF16)
+            gq[rows:, at] = (sin[:rows] + cos[rows:]).astype(BF16)
 
     def to_rows(value):
         stack = jnp.concatenate([value[:, k * C : (k + 1) * C] for k in range(kk)], axis=0)
         high = stack.astype(BF16).astype(F32)
         both = jnp.concatenate([high, stack - high], axis=1).astype(BF16)
-        return dot(vm["perm"][...], both).astype(BF16)
+        return dot(perm[...], both).astype(BF16)
 
     def from_rows(value):
         high = value.astype(BF16).astype(F32)
         both = jnp.concatenate([high, value - high], axis=1).astype(BF16)
-        moved = dot(vm["permt"][...], both)
+        moved = dot(permt[...], both)
         moved = moved[:, :C] + moved[:, C:]
         return jnp.concatenate([moved[k * PM : (k + 1) * PM] for k in range(kk)], axis=1)
 
     lane = lax.broadcasted_iota(jnp.int32, (PM, half), 1)
     first_k = (gx * ngy + gy) % blocks * kk
     doubling = jnp.where(lane // C + first_k == 0, 1.0, 2.0).astype(F32)
-
-    row = lax.broadcasted_iota(jnp.int32, (256, C), 0) % C
-    col = lax.broadcasted_iota(jnp.int32, (256, C), 1)
-    sel = (row == col).astype(F32).astype(BF16)
-    tall = dot(sel, wp_ref[...]).astype(BF16)
-    wide = lax.dot_general(tall, sel, (((1,), (1,)), ((), ())), preferred_element_type=F32)
-    br = lax.broadcasted_iota(jnp.int32, (256, 256), 0) // C
-    bc = lax.broadcasted_iota(jnp.int32, (256, 256), 1) // C
-    kw[...] = jnp.where(br == bc, wide, 0.0).astype(BF16)
-    bias = jnp.concatenate([bias_ref[...]] * 8, axis=1)
 
     loads["field"].wait()
     loads["ybd"].wait()
@@ -283,9 +278,39 @@
     for name in names:
         if name not in ("field", "ybd", "gz"):
             loads[name].wait()
+
+    def iota(shape, dim):
+        return lax.broadcasted_iota(jnp.int32, shape, dim)
+
+    def fill(ref, make):
+        one = make(iota(ref.shape, 0), iota(ref.shape, 1))
+        ref[...] = jnp.where(one, 1.0, 0.0).astype(BF16)
+
+    bits = kk.bit_length() - 1
+    fill(perm, lambda r, c: c == (r & (kk - 1)) * PM + (r >> bits))
+    fill(permt, lambda r, c: r == (c & (kk - 1)) * PM + (c >> bits))
+    fill(ei, lambda r, c: (r & 31) == (c >> 5))
+    fill(eo, lambda r, c: (r & 31) == (c & 31))
+    fill(ro, lambda r, c: (r & 31) == c)
+    fill(ri, lambda r, c: (r >> 5) == c)
+
+    row = iota((256, C), 0) & 31
+    col = iota((256, C), 1)
+    sel = (row == col).astype(F32).astype(BF16)
+    tall = dot(sel, vm["wp"][...]).astype(BF16)
+    wide = lax.dot_general(tall, sel, (((1,), (1,)), ((), ())), preferred_element_type=F32)
+    br = iota((256, 256), 0) >> 5
+    bc = iota((256, 256), 1) >> 5
+    kw[...] = jnp.where(br == bc, wide, 0.0).astype(BF16)
+    bias = jnp.concatenate([vm["bias"][...]] * 8, axis=1)
+
+    for b in range(4):
+        at = slice(b * 256, b * 256 + 256)
+        pre[:, at] = dot(vm["field"][:, at], kw[...]) + bias
+
     spec = gather_modes(0)
 
-    vexp[...] = dot(to_rows(spec), vm["ei"][...])
+    vexp[...] = dot(to_rows(spec), ei[...])
     for m in range(KX):
         a, b = slice(m * kk, (m + 1) * kk), slice(n + m * kk, n + (m + 1) * kk)
         vr, vi = vexp[a], vexp[b]
@@ -296,14 +321,13 @@
         red[a] = sum(pr[:, s * 128 : (s + 1) * 128] for s in range(8))
         red[b] = sum(pi[:, s * 128 : (s + 1) * 128] for s in range(8))
     high, low = split(red[...])
-    out = dot(high, vm["ro"][...]) + dot(low, vm["ro"][...])
+    out = dot(high, ro[...]) + dot(low, ro[...])
     scatter_modes(0, from_rows(out) * doubling)
     backward(0)
 
     @pl.loop(0, 4)
     def _(b):
-        mixed = dot(vm["field"][:, lanes(b)], kw[...])
-        v = dot(vm["ybt"][...], gq[:, lanes(b)]) + mixed + bias
+        v = dot(vm["ybt"][...], gq[:, lanes(b)]) + pre[:, lanes(b)]
         root = math.sqrt(2.0 / math.pi)
         square = v * v
         th = jnp.tanh(root * v * (1.0 + 0.044715 * square))
@@ -343,7 +367,7 @@
     precv[gx] = pbuf[...]
 
     spec = gather_modes(1) * doubling
-    hexp[...] = dot(to_rows(spec), vm["eo"][...])
+    hexp[...] = dot(to_rows(spec), eo[...])
     for m in range(KX):
         a, b = slice(m * kk, (m + 1) * kk), slice(n + m * kk, n + (m + 1) * kk)
         hr, hi = hexp[a], hexp[b]
@@ -352,7 +376,7 @@
         prod[a] = hr * wr + hi * wi
         prod[b] = hi * wr - hr * wi
     high, low = split(prod[...])
-    out = dot(high, vm["ri"][...]) + dot(low, vm["ri"][...])
+    out = dot(high, ri[...]) + dot(low, ri[...])
     scatter_modes(1, from_rows(out))
 
     got = precv.at[pl.ds(0, ngx - 1)]
@@ -381,12 +405,15 @@
 
     backward(1)
 
-    @pl.loop(0, 4)
-    def _(b):
+    gf_copies = []
+    for b in range(4):
+        at = pl.ds(b * 256, 256)
         back = lax.dot_general(
-            adj[:, lanes(b)], kw[...], (((1,), (1,)), ((), ())), preferred_element_type=F32
+            adj[:, at], kw[...], (((1,), (1,)), ((), ())), preferred_element_type=F32
         )
-        gf_out[:, lanes(b)] = (dot(vm["ybt"][...], gq[:, lanes(b)]) + back).astype(BF16)
+        gf[:, at] = (dot(vm["ybt"][...], gq[:, at]) + back).astype(BF16)
+        gf_copies.append(pltpu.make_async_copy(gf.at[:, at], gf_out.at[:, at], gf_sem.at[b]))
+        gf_copies[-1].start()
 
     got = precv2.at[pl.ds(0, ngy - 1)]
     pltpu.make_async_copy(got, got, p_recv.at[1]).wait()
@@ -394,8 +421,21 @@
     gp_out[...] = total[:C, :C]
     gb_out[...] = total[C : C + 1, :C]
     gs_copy.wait()
+    for copy in gf_copies:
+        copy.wait()
     for copy in pending:
         copy.wait_send()
+
+
+def hand_over(*refs):
+    sem = refs[-1]
+    count = len(refs) // 2
+    copies = []
+    for i in range(count):
+        copies.append(pltpu.make_async_copy(refs[i], refs[count + i], sem.at[i]))
+        copies[-1].start()
+    for copy in copies:
+        copy.wait()
 
 
 def on_device(ngx, ngy, field_input, cotangent, spectral_weight, point_weight, point_bias):
@@ -413,6 +453,8 @@
     for name in TABLES:
         arrays[name] = consts[name]
     arrays["cot"] = cotangent.reshape(cells, depth)
+    arrays["wp"] = point_weight
+    arrays["bias"] = point_bias.reshape(1, C)
     names = tuple(arrays)
     local = [
         pltpu.VMEM(a.shape[1:] if k in BY_GY else a.shape, a.dtype) for k, a in arrays.items()
@@ -422,7 +464,7 @@
     vmem = pl.BlockSpec(memory_space=pltpu.VMEM)
     hbm = pl.BlockSpec(memory_space=pl.ANY)
     dma = pltpu.SemaphoreType.DMA
-    grad_field, grad_spectral, grad_point, grad_bias = pl.pallas_call(
+    results = pl.pallas_call(
         functools.partial(kernel, ngx, ngy, rx, ry, kk, names),
         out_shape=(
             jax.ShapeDtypeStruct((cells, depth), BF16),
@@ -430,8 +472,8 @@
             jax.ShapeDtypeStruct((C, C), F32),
             jax.ShapeDtypeStruct((1, C), F32),
         ),
-        in_specs=[hbm] * len(names) + [vmem, vmem],
-        out_specs=(vmem, hbm, vmem, vmem),
+        in_specs=[pl.BlockSpec(memory_space=pltpu.HBM)] * len(names),
+        out_specs=(hbm, hbm, vmem, vmem),
         scratch_shapes=local
         + [
             pltpu.VMEM((2 * rows, depth), BF16),
@@ -457,8 +499,18 @@
             pltpu.VMEM((ngx, C + 8, 128), F32),
             pltpu.VMEM((C + 8, 128), F32),
             pltpu.VMEM((ngy, C + 8, 128), F32),
+            pltpu.VMEM((2 * rows, KZ * C), BF16),
+            pltpu.VMEM((cells, depth), F32),
+            pltpu.VMEM((cells, depth), BF16),
+            pltpu.VMEM((n2, n2), BF16),
+            pltpu.VMEM((n2, n2), BF16),
+            pltpu.VMEM((2 * C, C * C), BF16),
+            pltpu.VMEM((2 * C, C * C), BF16),
+            pltpu.VMEM((128, C), BF16),
+            pltpu.VMEM((C * C, C), BF16),
             dma((len(names),)),
             dma,
+            dma((4,)),
             dma((2, ngy, ngx - 1)),
             dma((2, ngy)),
             dma((2, ngy)),
@@ -473,7 +525,14 @@
         compiler_params=pltpu.CompilerParams(
             collective_id=0, has_side_effects=True, vmem_limit_bytes=52 * 1024 * 1024
         ),
-    )(*arrays.values(), point_weight, point_bias.reshape(1, C))
+    )(*arrays.values())
+    grad_field, grad_spectral, grad_point, grad_bias = pl.pallas_call(
+        hand_over,
+        out_shape=tuple(jax.ShapeDtypeStruct(r.shape, r.dtype) for r in results),
+        in_specs=[hbm] * 4,
+        out_specs=(hbm,) * 4,
+        scratch_shapes=[dma((4,))],
+    )(*results)
     return (
         grad_field.reshape(rx, ry, depth),
         grad_spectral,

time: 87 us -> 169 us (1.94)
  Pallas kernels: 70.9 us -> 163 us
  local copies, waits for them, and re-layouts: 14.8 us -> 4.92 us
    pallas_call x0 -> x1, Pallas kernels: none -> 96.9 us  [on_device(): pl.pallas_call(hand_over, out_shape=tuple((jax.ShapeDtypeStruct(r.shape,...]
    unnamed x24 -> x14, local copies, waits for them, and re-layouts: 14.8 us -> 4.92 us
    pallas_call x1, Pallas kernels: 70.9 us -> 65.6 us  [on_device(): pl.pallas_call(functools.partial(kernel, ngx, ngy, rx, ry, kk, names), ou...]
where the time goes in v1:
time: 169 us; the launch traced here: 168 us
  Pallas kernels  163 us (96%)
  local copies, waits for them, and re-layouts  4.92 us (3%)
    pallas_call x1, Pallas kernels, on_device(): pl.pallas_call(hand_over, out_shape=tuple((jax.ShapeDtypeStruct(r.shape,...  96.9 us
    pallas_call x1, Pallas kernels, on_device(): pl.pallas_call(functools.partial(kernel, ngx, ngy, rx, ry, kk, names), ou...  65.6 us
    unnamed x14, local copies, waits for them, and re-layouts  4.92 us

profile of v1, /device:TPU:0, one launch (start us, length us, event | category | flops | bytes accessed | tf_op | source)
XLA Modules:
  0.0 168.1 jit_solution(8508146028301893759)
XLA Ops:
  0.6 0.0 copy-start.2
  0.6 0.7 copy-done.2
  1.4 0.0 copy-start.3
  1.4 0.7 copy-done.3
  2.1 0.0 copy-start.4
  2.1 0.7 copy-done.4
  2.8 0.0 copy-start.5
  2.8 0.7 copy-done.5
  3.4 65.6 %shard_map.138 = (bf16[512,1024]{1,0:T(8,128)(2,1)S(1)}, f32[16,32768]{1,0:T(8,128)}, f32[32,32]{1,0:T(8,128)S(1)}, f32[1,32]{1,0:T(1,128)S(1)}) custom-call(bf16[512,1024]{1,0:T(8,128)(2,1)} %bitcast.6, bf16[4,256,512]{2,1,0:T(8,128)(2,1)} %constant.12.clone.refs_1_, bf16[1024,1024]{1,0:T(8,128)(2,1)} %constant.13.clone.refs_2_, ...), custom_call_target="tpu_custom_call" | custom-call | tf_op jit(solution)/shard_map/pallas_call | solution.py:467
  69.0 0.0 copy-start
  69.0 1.0 copy-done
  70.0 0.0 copy-start.1
  70.0 0.6 copy-done.1
  70.6 0.0 copy-start.6
  70.6 0.6 copy-done.6
  71.2 96.9 %shard_map.139 = (bf16[512,1024]{1,0:T(8,128)(2,1)}, f32[16,32768]{1,0:T(8,128)}, f32[32,32]{1,0:T(8,128)}, f32[1,32]{1,0:T(1,128)}) custom-call(bf16[512,1024]{1,0:T(8,128)(2,1)} %copy-done, f32[16,32768]{1,0:T(8,128)} %get-tuple-element.13.refs_1_, f32[32,32]{1,0:T(8,128)} %copy-done.1, f32[1,32]{1,0:T(1,128)} %copy-done.6), custom_call_target="tpu_custom_call" | custom-call | tf_op jit(solution)/shard_map/pallas_call | solution.py:529
Async XLA Ops:
  0.6 0.7 copy-start.2
  1.4 0.7 copy-start.3
  2.1 0.7 copy-start.4
  2.8 0.7 copy-start.5
  69.0 1.0 copy-start
  70.0 0.6 copy-start.1
  70.6 0.6 copy-start.6

commit v2 on v1

v2 whole, which is shorter than its diff:
```python
import functools
import math

import jax
import jax.numpy as jnp
import numpy as np
from jax import lax
from jax.experimental import pallas as pl
from jax.experimental.pallas import tpu as pltpu
from jax.sharding import PartitionSpec as P

C = 32
KX = 16
KY = 16
KZ = 16
NZ = 32
PM = 2 * KX
F32 = jnp.float32
BF16 = jnp.bfloat16
MESH = pl.DeviceIdType.MESH


def modes(count, length):
    position = np.arange(count)
    return np.where(position < count // 2, position, length - count + position)


def angles(positions, wavenumbers, length):
    steps = positions[:, None] * wavenumbers[None, :] % length
    return 2.0 * math.pi / length * steps.astype(np.float64)


def tables(ngx, ngy, rows_x, rows_y, kk):
    full_x, full_y = ngx * rows_x, ngy * rows_y
    scale = 1.0 / math.sqrt(full_x * full_y * NZ)
    tz = angles(np.arange(NZ), np.arange(KZ), NZ)
    eye = np.eye(C, dtype=np.float32)
    to_modes = np.concatenate(
        [np.kron(f(tz).astype(np.float32), eye) for f in (np.cos, np.sin)], 1
    )
    from_modes = np.concatenate(
        [np.kron(f(tz).astype(np.float32).T, eye) for f in (np.cos, np.sin)], 1
    )
    ty = angles(np.arange(full_y), modes(KY, full_y), full_y).reshape(ngy, rows_y, KY)
    ytab = np.stack([np.cos(ty), -np.sin(ty)], 1).transpose(0, 1, 3, 2)
    ybd = np.einsum("gqjy,xw->gqjxwy", ytab, np.eye(rows_x))
    ybd = ybd.reshape(ngy, 2 * KY * rows_x, rows_x * rows_y)
    tx = angles(np.arange(full_x), modes(KX, full_x), full_x).T
    cx, sx = np.cos(tx) * scale, np.sin(tx) * scale
    xf = np.concatenate(
        [np.concatenate([cx, sx], 1), np.concatenate([-sx, cx], 1)], 0
    )
    bf = lambda a: np.ascontiguousarray(a).astype(jnp.bfloat16)

    def three(a):
        high = bf(a)
        low = bf(a - high.astype(np.float64))
        wide = np.concatenate([high, high, low], 1)
        return np.pad(wide, ((0, -len(wide) % 16), (0, to_modes.shape[1] - wide.shape[1])))

    return dict(
        ybd=jnp.asarray(bf(ybd)),
        gz=jnp.asarray(np.concatenate([bf(to_modes), three(xf), three(xf.T)], 0)),
        ybt=jnp.asarray(bf(ybd.transpose(0, 2, 1))),
        hz=jnp.asarray(bf(from_modes)),
    )


TABLES = ["ybd", "gz", "hz"]
BY_GY = ("ybd", "ybt")
VMEM_LIMIT = 61 * 1024 * 1024


def dot(a, b):
    return jnp.dot(a, b, preferred_element_type=F32)


def dot3(table, b):
    high, low = split(b)
    return dot(table, jnp.concatenate([high, low, high], axis=0))


def split(a):
    high = a.astype(BF16)
    return high, (a - high.astype(F32)).astype(BF16)


def iota(shape, dim):
    return lax.broadcasted_iota(jnp.int32, shape, dim)


def fill(ref, make):
    one = make(iota(ref.shape, 0), iota(ref.shape, 1))
    ref[...] = jnp.where(one, 1.0, 0.0).astype(BF16)


def over_out(r, c):
    return (r & 31) == (c >> 5)


def over_in(r, c):
    return (r & 31) == (c & 31)


def kernel(ngx, ngy, rx, ry, kk, parts, names, *refs):
    it = iter(refs)
    hbm = {name: next(it) for name in names}
    vr_out, hr_out, gq_out, adj_out, kw_out, tot_out = (next(it) for _ in range(6))
    vm = {name: next(it) for name in names}
    (ybuf, zout, recv1, send2, recv2, zs, recvs, fs, fin, gq, vexp, hexp, red, prod,
     adj, vrow, hrow, acc, accb, kw, pbuf, precv, pbuf2, precv2, f2, pre, gacc, tot, wf,
     perm, permt, ei, eo, ro, ri) = (next(it) for _ in range(35))
    (in_sem, out_sem, s1_send, s1_recv, s2_send, s2_recv, g_send, g_recv, f_send, f_recv,
     p_send, p_recv) = (next(it) for _ in range(12))

    gx, gy = lax.axis_index("gx"), lax.axis_index("gy")
    nx = ngx * rx
    kc = kk // parts
    half = kc * C
    width = 2 * half
    blocks = KZ // kc
    shares = KZ // kk
    n = KX * kc
    modes_in = KZ * C
    xf0, xs0 = NZ * C, NZ * C + PM
    scale = 1.0 / math.sqrt(nx * ngy * ry * NZ)

    loads = {}
    for i, name in enumerate(names):
        src = hbm[name].at[gy] if name in BY_GY else hbm[name]
        loads[name] = pltpu.make_async_copy(src, vm[name], in_sem.at[i])
        loads[name].start()

    barrier = pltpu.get_barrier_semaphore()
    for e in range(1, ngx):
        pl.semaphore_signal(barrier, inc=1, device_id={"gx": lax.rem(gx + e, ngx)}, device_id_type=MESH)
    for d in range(1, ngy):
        pl.semaphore_signal(barrier, inc=1, device_id={"gy": lax.rem(gy + d, ngy)}, device_id_type=MESH)

    def slab(ref, owner, h):
        rows = pl.ds(pl.multiple_of(owner // shares * rx, rx), rx)
        if shares == 1:
            return ref.at[rows, pl.ds(h * width, width)]
        block = owner % shares * parts + h
        return ref.at[rows, pl.ds(pl.multiple_of(block * width, width), width)]

    def lanes(b):
        return pl.ds(pl.multiple_of(b * 256, 256), 256)

    chips = ngx // 2
    chip, core = gx // 2, gx % 2
    steps = [(c, k) for c in range(1, chips) for k in range(2)] + [(0, 1)]
    peers = [lax.rem(chip + c, chips) * 2 + lax.rem(core + k, 2) for c, k in steps]
    way = 1 - 2 * (gy // (ngy // 2))

    def along(d):
        return lax.rem(gy + way * d + ngy, ngy)

    far_first = list(range(ngy - 1, -1, -1))
    pending = []

    rows = KY * rx

    def forward(t, u):
        for b in range(4):
            at = slice(b * 256, b * 256 + 256)
            ybuf[:, at] = dot(vm["ybd"][...], u[:, at]).astype(BF16)
        if t == 0:
            loads["gz"].wait()
        for b in range(2):
            cos = dot(ybuf[...], vm["gz"][: NZ * C, b * 256 : b * 256 + 256])
            sin = dot(ybuf[...], vm["gz"][: NZ * C, modes_in + b * 256 : modes_in + b * 256 + 256])
            real = cos[:rows] + sin[rows:]
            imag = cos[rows:] - sin[:rows]
            part = min(half, 256)
            for i in range(256 // part):
                lane0 = b * 256 + i * part
                at = lane0 // half * width + lane0 % half
                zout[t, :, at : at + part] = real[:, i * part : (i + 1) * part]
                zout[t, :, at + half : at + half + part] = imag[:, i * part : (i + 1) * part]
            if t == 0 and b == 0:
                pl.semaphore_wait(barrier, ngx + ngy - 2)
            if parts == 2:
                send_cells(t, b)
        if parts == 1:
            send_cells(t, 0)

    mine = pl.ds(pl.multiple_of(gx * rx, rx), rx)

    def send_cells(t, h):
        for d in far_first:
            g = along(d)
            for e, to in enumerate(peers):
                copy = pltpu.make_async_remote_copy(
                    src_ref=slab(zout.at[t], to * ngy + g, h),
                    dst_ref=recv1.at[t, h, g, mine],
                    send_sem=s1_send.at[t, h, d, e],
                    recv_sem=s1_recv.at[t, h, g],
                    device_id={"gx": to},
                    device_id_type=MESH,
                )
                copy.start()
                pending.append(copy)
            recv1[t, h, g, mine] = slab(zout.at[t], gx * ngy + g, h)[...]

    def send_sums(t, h):
        for d in far_first:
            g = along(d)
            got = recv1.at[t, h, g, pl.ds(0, (ngx - 1) * rx)]
            pltpu.make_async_copy(got, got, s1_recv.at[t, h, g]).wait()
            both = jnp.concatenate([recv1[t, h, g, :, :half], recv1[t, h, g, :, half:]], axis=0)
            value = dot3(vm["gz"][xf0 : xf0 + PM, : 6 * nx], both)
            if d == 0:
                recv2[t, h, gy] = value
            else:
                send2[t, h, d] = value
                copy = pltpu.make_async_remote_copy(
                    src_ref=send2.at[t, h, d],
                    dst_ref=recv2.at[t, h, gy],
                    send_sem=s2_send.at[t, h, d],
                    recv_sem=s2_recv.at[t, h],
                    device_id={"gy": g},
                    device_id_type=MESH,
                )
                copy.start()
                pending.append(copy)

    def add_sums(t, h):
        got = recv2.at[t, h, pl.ds(0, ngy - 1)]
        pltpu.make_async_copy(got, got, s2_recv.at[t, h]).wait()
        total = recv2[t, h, 0]
        for g in range(1, ngy):
            total = total + recv2[t, h, g]
        return total

    def send_modes(t, h, value):
        zs[t, h] = value
        for d in range(ngy - 1, 0, -1):
            copy = pltpu.make_async_remote_copy(
                src_ref=zs.at[t, h],
                dst_ref=recvs.at[t, h, gy],
                send_sem=g_send.at[t, h, d],
                recv_sem=g_recv.at[t, h, gy],
                device_id={"gy": along(d)},
                device_id_type=MESH,
            )
            copy.start()
            pending.append(copy)
        return_cells(t, h, 0, value)

    def return_cells(t, h, d, block):
        g = along(d)
        if d:
            got = recvs.at[t, h, g]
            pltpu.make_async_copy(got, got, g_recv.at[t, h, g]).wait()
            block = recvs[t, h, g]
        both = dot3(vm["gz"][xs0 : xs0 + 2 * nx, : 3 * PM], block)
        fs[t, h, g, :, :half] = both[:nx]
        fs[t, h, g, :, half:] = both[nx:]
        owner = gx * ngy + g
        for e, to in enumerate(peers):
            copy = pltpu.make_async_remote_copy(
                src_ref=fs.at[t, h, g, pl.ds(pl.multiple_of(to * rx, rx), rx)],
                dst_ref=slab(fin.at[t], owner, h),
                send_sem=f_send.at[t, h, d, e],
                recv_sem=f_recv.at[t, h],
                device_id={"gx": to},
                device_id_type=MESH,
            )
            copy.start()
            pending.append(copy)
        slab(fin.at[t], owner, h)[...] = fs[t, h, g, mine]

    def exchange(t, mix):
        for h in range(parts):
            send_sums(t, h)
        for h in range(parts):
            send_modes(t, h, mix(h, add_sums(t, h)))
        for h in range(parts):
            for d in range(1, ngy):
                return_cells(t, h, d, None)

    def backward(t):
        per = modes_in // parts
        for h in range(parts):
            got = fin.at[t, pl.ds(0, rows // ngx * (ngx - 1)), pl.ds(h * 2 * per, 2 * per)]
            pltpu.make_async_copy(got, got, f_recv.at[t, h]).wait()
            for kb in range(h * blocks // parts, (h + 1) * blocks // parts):
                at, to = kb * width, slice(kb * half, (kb + 1) * half)
                f2[:rows, to] = fin[t, :, at : at + half].astype(BF16)
                f2[rows:, to] = fin[t, :, at + half : at + width].astype(BF16)
            k = slice(h * per, (h + 1) * per)
            for b in range(4):
                at = slice(b * 256, b * 256 + 256)
                cos = dot(f2[:, k], vm["hz"][k, at])
                sin = dot(f2[:, k], vm["hz"][k, NZ * C + b * 256 : NZ * C + b * 256 + 256])
                real, imag = cos[:rows] - sin[rows:], sin[:rows] + cos[rows:]
                if h:
                    real, imag = real + gacc[:rows, at], imag + gacc[rows:, at]
                if h == parts - 1:
                    gq[:rows, at] = real.astype(BF16)
                    gq[rows:, at] = imag.astype(BF16)
                else:
                    gacc[:rows, at] = real
                    gacc[rows:, at] = imag

    def to_rows(value):
        stack = jnp.concatenate([value[:, k * C : (k + 1) * C] for k in range(kc)], axis=0)
        high = stack.astype(BF16).astype(F32)
        both = jnp.concatenate([high, stack - high], axis=1).astype(BF16)
        return dot(perm[...], both).astype(BF16)

    def from_rows(value):
        high = value.astype(BF16).astype(F32)
        both = jnp.concatenate([high, value - high], axis=1).astype(BF16)
        moved = dot(permt[...], both)
        moved = moved[:, :C] + moved[:, C:]
        return jnp.concatenate([moved[k * PM : (k + 1) * PM] for k in range(kc)], axis=1)

    lane = iota((PM, half), 1)
    first_k = (gx * ngy + gy) % shares * kk

    def doubling(h):
        return jnp.where((lane >> 5) + first_k + h * kc == 0, 1.0, 2.0).astype(F32)

    loads["field"].wait()
    loads["ybd"].wait()
    forward(0, vm["field"])
    for name in names:
        if name not in ("field", "ybd", "gz"):
            loads[name].wait()

    bits = kc.bit_length() - 1
    fill(perm, lambda r, c: c == (r & (kc - 1)) * PM + (r >> bits))
    fill(permt, lambda r, c: r == (c & (kc - 1)) * PM + (c >> bits))
    fill(ei, over_out)
    fill(eo, over_in)
    fill(ro, lambda r, c: (r & 31) == c)
    fill(ri, lambda r, c: (r >> 5) == c)

    row = iota((256, C), 0) & 31
    col = iota((256, C), 1)
    sel = (row == col).astype(F32).astype(BF16)
    tall = dot(sel, vm["wp"][...]).astype(BF16)
    wide = lax.dot_general(tall, sel, (((1,), (1,)), ((), ())), preferred_element_type=F32)
    br = iota((256, 256), 0) >> 5
    bc = iota((256, 256), 1) >> 5
    kw[...] = jnp.where(br == bc, wide, 0.0).astype(BF16)
    bias = jnp.concatenate([vm["bias"][...]] * 8, axis=1)

    for b in range(4):
        at = slice(b * 256, b * 256 + 256)
        pre[:, at] = dot(vm["field"][:, at], kw[...]) + bias

    for i in range(2 * KX):
        at = slice(i * C * C, (i + 1) * C * C)
        wf[:, at] = vm["weight"][:, at].astype(F32)

    def weights(h, m):
        k = slice(h * kc, (h + 1) * kc)
        return wf[k, m * 2048 : m * 2048 + 1024], wf[k, m * 2048 + 1024 : m * 2048 + 2048]

    def pair(m):
        return slice(m * kc, (m + 1) * kc), slice(n + m * kc, n + (m + 1) * kc)

    def mix_out(h, spec):
        vrow[h] = to_rows(spec)
        vexp[...] = dot(vrow[h], ei[...])
        for m in range(KX):
            a, b = pair(m)
            vr, vi = vexp[a], vexp[b]
            wr, wi = weights(h, m)
            pr = vr * wr - vi * wi
            pi = vr * wi + vi * wr
            red[a] = sum(pr[:, s * 128 : (s + 1) * 128] for s in range(8))
            red[b] = sum(pi[:, s * 128 : (s + 1) * 128] for s in range(8))
        high, low = split(red[...])
        out = dot(high, ro[...]) + dot(low, ro[...])
        return from_rows(out) * doubling(h)

    def mix_in(h, spec):
        hrow[h] = to_rows(spec * doubling(h))
        hexp[...] = dot(hrow[h], eo[...])
        for m in range(KX):
            a, b = pair(m)
            hr, hi = hexp[a], hexp[b]
            wr, wi = weights(h, m)
            prod[a] = hr * wr + hi * wi
            prod[b] = hi * wr - hr * wi
        high, low = split(prod[...])
        out = dot(high, ri[...]) + dot(low, ri[...])
        return from_rows(out)

    results = []

    def give(src, dst):
        results.append(pltpu.make_async_copy(src, dst, out_sem.at[len(results)]))
        results[-1].start()

    give(kw, kw_out)
    exchange(0, mix_out)
    give(vrow, vr_out)
    backward(0)

    @pl.loop(0, 4)
    def _(b):
        v = dot(vm["ybt"][...], gq[:, lanes(b)]) + pre[:, lanes(b)]
        root = math.sqrt(2.0 / math.pi)
        square = v * v
        th = jnp.tanh(root * v * (1.0 + 0.044715 * square))
        slope = 0.5 * (1.0 + th) + 0.5 * v * (1.0 - th * th) * (
            root * (1.0 + 3 * 0.044715 * square)
        )
        adj[:, lanes(b)] = (vm["cot"][:, lanes(b)].astype(F32) * slope).astype(BF16)

    give(adj, adj_out)
    forward(1, adj)

    acc[...] = jnp.zeros_like(acc)
    accb[...] = jnp.zeros_like(accb)
    ones = jnp.ones((16, rx * ry), BF16)

    @pl.loop(0, 4)
    def _(b):
        block = adj[:, lanes(b)]
        acc[...] += lax.dot_general(
            vm["field"][:, lanes(b)], block, (((0,), (0,)), ((), ())), preferred_element_type=F32
        )
        accb[...] += dot(ones, block)

    pbuf[...] = jnp.zeros_like(pbuf)
    pbuf[:C, :C] = sum(acc[i * C : (i + 1) * C, i * C : (i + 1) * C] for i in range(8)) * scale
    pbuf[C:, :C] = sum(accb[:8, i * C : (i + 1) * C] for i in range(8)) * scale
    for e in range(1, ngx):
        copy = pltpu.make_async_remote_copy(
            src_ref=pbuf,
            dst_ref=precv.at[gx],
            send_sem=p_send.at[e],
            recv_sem=p_recv.at[0],
            device_id={"gx": lax.rem(gx + e, ngx)},
            device_id_type=MESH,
        )
        copy.start()
        pending.append(copy)
    precv[gx] = pbuf[...]

    exchange(1, mix_in)
    give(hrow, hr_out)

    got = precv.at[pl.ds(0, ngx - 1)]
    pltpu.make_async_copy(got, got, p_recv.at[0]).wait()
    pbuf2[...] = sum(precv[i] for i in range(ngx))
    for d in range(1, ngy):
        copy = pltpu.make_async_remote_copy(
            src_ref=pbuf2,
            dst_ref=precv2.at[gy],
            send_sem=p_send.at[ngx + d],
            recv_sem=p_recv.at[1],
            device_id={"gy": lax.rem(gy + d, ngy)},
            device_id_type=MESH,
        )
        copy.start()
        pending.append(copy)
    precv2[gy] = pbuf2[...]

    backward(1)
    give(gq, gq_out)
    got = precv2.at[pl.ds(0, ngy - 1)]
    pltpu.make_async_copy(got, got, p_recv.at[1]).wait()
    tot[...] = sum(precv2[i] for i in range(ngy))
    give(tot, tot_out)
    for copy in results:
        copy.wait()
    for copy in pending:
        copy.wait_send()


def finish(scale, kk, parts, *refs):
    (vr_in, hr_in, gq_in, adj_in, kw_in, tot_in, ybt_in, gf_out, gs_out, gp_out, gb_out,
     vrow, hrow, gq, adj, kw, tot, ybt, gf, gs, gp, gb, vexp, hexp, ei, eo, in_sem,
     out_sem) = refs
    kc = kk // parts
    n = KX * kc
    loads = [
        pltpu.make_async_copy(src, dst, in_sem.at[i])
        for i, (src, dst) in enumerate(
            [(vr_in, vrow), (hr_in, hrow), (gq_in, gq), (adj_in, adj), (kw_in, kw),
             (tot_in, tot), (ybt_in.at[lax.axis_index("gy")], ybt)]
        )
    ]
    for load in loads:
        load.start()
    fill(ei, over_out)
    fill(eo, over_in)
    results = []

    def give(src, dst):
        results.append(pltpu.make_async_copy(src, dst, out_sem.at[len(results)]))
        results[-1].start()

    loads[0].wait()
    loads[1].wait()
    for h in range(parts):
        k = slice(h * kc, (h + 1) * kc)
        vexp[...] = dot(vrow[h], ei[...])
        hexp[...] = dot(hrow[h], eo[...])
        for m in range(KX):
            a, b = slice(m * kc, (m + 1) * kc), slice(n + m * kc, n + (m + 1) * kc)
            vr, vi, hr, hi = vexp[a], vexp[b], hexp[a] * scale, hexp[b] * scale
            gs[k, m * 2048 : m * 2048 + 1024] = vr * hr + vi * hi
            gs[k, m * 2048 + 1024 : m * 2048 + 2048] = vr * hi - vi * hr
        if parts == 1:
            give(gs, gs_out)
        else:
            give(gs.at[pl.ds(h * kc, kc)], gs_out.at[pl.ds(h * kc, kc)])
    for load in loads[2:]:
        load.wait()
    gp[...] = tot[:C, :C]
    gb[...] = tot[C : C + 1, :C]
    give(gp, gp_out)
    give(gb, gb_out)
    for b in range(4):
        at = pl.ds(b * 256, 256)
        back = lax.dot_general(
            adj[:, at], kw[...], (((1,), (1,)), ((), ())), preferred_element_type=F32
        )
        gf[:, at] = (dot(ybt[...], gq[:, at]) + back).astype(BF16)
        give(gf.at[:, at], gf_out.at[:, at])
    for copy in results:
        copy.wait()


def on_device(ngx, ngy, field_input, cotangent, spectral_weight, point_weight, point_bias):
    rx, ry, depth = field_input.shape
    kk = spectral_weight.shape[0]
    cells = rx * ry
    nx = rx * ngx
    parts = 2 if kk == KZ else 1
    kc = kk // parts
    half, width = kc * C, 2 * kc * C
    arrays = dict(field=field_input.reshape(cells, depth))
    consts = tables(ngx, ngy, rx, ry, kk)
    arrays["ybd"] = consts["ybd"]
    arrays["gz"] = consts["gz"]
    arrays["weight"] = spectral_weight
    for name in TABLES:
        arrays[name] = consts[name]
    arrays["ybt"] = consts["ybt"]
    arrays["cot"] = cotangent.reshape(cells, depth)
    arrays["wp"] = point_weight
    arrays["bias"] = point_bias.reshape(1, C)
    names = tuple(arrays)
    local = [
        pltpu.VMEM(a.shape[1:] if k in BY_GY else a.shape, a.dtype) for k, a in arrays.items()
    ]
    rows = KY * rx
    n2 = PM * kc
    hbm = pl.BlockSpec(memory_space=pltpu.HBM)
    dma = pltpu.SemaphoreType.DMA
    rows_type = jax.ShapeDtypeStruct((parts, n2, 2 * C), BF16)
    between = (
        rows_type,
        rows_type,
        jax.ShapeDtypeStruct((2 * rows, depth), BF16),
        jax.ShapeDtypeStruct((cells, depth), BF16),
        jax.ShapeDtypeStruct((256, 256), BF16),
        jax.ShapeDtypeStruct((C + 8, 128), F32),
    )

    def room(types):
        return [pltpu.VMEM(a.shape, a.dtype) for a in types]

    kept = pl.pallas_call(
        functools.partial(kernel, ngx, ngy, rx, ry, kk, parts, names),
        out_shape=between,
        in_specs=[hbm] * len(names),
        out_specs=(hbm,) * len(between),
        scratch_shapes=local
        + [
            pltpu.VMEM((2 * rows, depth), BF16),
            pltpu.VMEM((2, rows, depth), F32),
            pltpu.VMEM((2, parts, ngy, nx, width), F32),
            pltpu.VMEM((2, parts, ngy, PM, half), F32),
            pltpu.VMEM((2, parts, ngy, PM, half), F32),
            pltpu.VMEM((2, parts, PM, half), F32),
            pltpu.VMEM((2, parts, ngy, PM, half), F32),
            pltpu.VMEM((2, parts, ngy, nx, width), F32),
            pltpu.VMEM((2, rows, depth), F32),
            pltpu.VMEM((2 * rows, depth), BF16),
            pltpu.VMEM((n2, C * C), F32),
            pltpu.VMEM((n2, C * C), F32),
            pltpu.VMEM((n2, 128), F32),
            pltpu.VMEM((n2, C * C), F32),
            pltpu.VMEM((cells, depth), BF16),
            pltpu.VMEM((parts, n2, 2 * C), BF16),
            pltpu.VMEM((parts, n2, 2 * C), BF16),
            pltpu.VMEM((256, 256), F32),
            pltpu.VMEM((16, 256), F32),
            pltpu.VMEM((256, 256), BF16),
            pltpu.VMEM((C + 8, 128), F32),
            pltpu.VMEM((ngx, C + 8, 128), F32),
            pltpu.VMEM((C + 8, 128), F32),
            pltpu.VMEM((ngy, C + 8, 128), F32),
            pltpu.VMEM((2 * rows, KZ * C), BF16),
            pltpu.VMEM((cells, depth), F32),
            pltpu.VMEM((2 * rows, depth), F32),
            pltpu.VMEM((C + 8, 128), F32),
            pltpu.VMEM(spectral_weight.shape, F32),
            pltpu.VMEM((n2, n2), BF16),
            pltpu.VMEM((n2, n2), BF16),
            pltpu.VMEM((2 * C, C * C), BF16),
            pltpu.VMEM((2 * C, C * C), BF16),
            pltpu.VMEM((128, C), BF16),
            pltpu.VMEM((C * C, C), BF16),
            dma((len(names),)),
            dma((len(between),)),
            dma((2, parts, ngy, ngx - 1)),
            dma((2, parts, ngy)),
            dma((2, parts, ngy)),
            dma((2, parts)),
            dma((2, parts, ngy)),
            dma((2, parts, ngy)),
            dma((2, parts, ngy, ngx - 1)),
            dma((2, parts)),
            dma((ngx + ngy,)),
            dma((2,)),
        ],
        compiler_params=pltpu.CompilerParams(
            collective_id=0, has_side_effects=True, vmem_limit_bytes=VMEM_LIMIT
        ),
    )(*arrays.values())
    wanted = (
        jax.ShapeDtypeStruct((cells, depth), BF16),
        jax.ShapeDtypeStruct(spectral_weight.shape, F32),
        jax.ShapeDtypeStruct((C, C), F32),
        jax.ShapeDtypeStruct((1, C), F32),
    )
    scale = 1.0 / math.sqrt(nx * ngy * ry * NZ)
    grad_field, grad_spectral, grad_point, grad_bias = pl.pallas_call(
        functools.partial(finish, scale, kk, parts),
        out_shape=wanted,
        in_specs=[hbm] * (len(between) + 1),
        out_specs=(hbm,) * len(wanted),
        scratch_shapes=room(between)
        + [pltpu.VMEM(consts["ybt"].shape[1:], BF16)]
        + room(wanted)
        + [
            pltpu.VMEM((n2, C * C), F32),
            pltpu.VMEM((n2, C * C), F32),
            pltpu.VMEM((2 * C, C * C), BF16),
            pltpu.VMEM((2 * C, C * C), BF16),
            dma((len(between) + 1,)),
            dma((parts + 6,)),
        ],
        compiler_params=pltpu.CompilerParams(vmem_limit_bytes=VMEM_LIMIT),
    )(*kept, consts["ybt"])
    return (
        grad_field.reshape(rx, ry, depth),
        grad_spectral,
        grad_point,
        grad_bias.reshape(C),
    )


def solution(mesh):
    return jax.shard_map(
        functools.partial(on_device, mesh.shape["gx"], mesh.shape["gy"]),
        mesh=mesh,
        in_specs=(
            P(("groups", "gx"), "gy", None),
            P(("groups", "gx"), "gy", None),
            P(("gx", "gy"), None),
            P(),
            P(),
        ),
        out_specs=(
            P(("groups", "gx"), "gy", None),
            P(("groups", "gx", "gy"), None),
            P("groups", None),
            P("groups"),
        ),
        check_vma=False,
    )
```

time: 169 us -> 58.8 us (0.35)
  Pallas kernels: 163 us -> 58 us
  local copies, waits for them, and re-layouts: 4.92 us -> 0 us
    pallas_call x2, Pallas kernels: 163 us -> 58 us  [the longest x1 54.6 us: on_device(): pl.pallas_call(functools.partial(kernel, ngx, ngy, rx, ry, kk, parts, nam...]
    unnamed x14 -> x0, local copies, waits for them, and re-layouts: 4.92 us -> none
where the time goes in v2:
time: 58.8 us; the launch traced here: 58.7 us
  Pallas kernels  58 us (99%)
  between operations  0.64 us (1%)
    pallas_call x1, Pallas kernels, on_device(): pl.pallas_call(functools.partial(kernel, ngx, ngy, rx, ry, kk, parts, nam...  54.6 us
    pallas_call x1, Pallas kernels, on_device(): pl.pallas_call(functools.partial(finish, scale, kk, parts), out_shape=wan...  3.45 us

profile of v2, /device:TPU:0, one launch (start us, length us, event | category | flops | bytes accessed | tf_op | source)
XLA Modules:
  0.0 58.7 jit_solution(4003293923659642856)
XLA Ops:
  0.6 54.6 %shard_map.120 = (bf16[2,256,64]{2,1,0:T(8,128)(2,1)}, bf16[2,256,64]{2,1,0:T(8,128)(2,1)}, bf16[256,1024]{1,0:T(8,128)(2,1)}, bf16[512,1024]{1,0:T(8,128)(2,1)}...) custom-call(bf16[512,1024]{1,0:T(8,128)(2,1)} %bitcast.5, bf16[4,256,512]{2,1,0:T(8,128)(2,1)} %constant.8.clone.refs_1_, ...), custom_call_target="tpu_custom_call" | custom-call | tf_op jit(solution)/shard_map/pallas_call | solution.py:573
  55.2 3.4 %shard_map.121 = (bf16[512,1024]{1,0:T(8,128)(2,1)}, f32[16,32768]{1,0:T(8,128)}, f32[32,32]{1,0:T(8,128)}, f32[1,32]{1,0:T(1,128)}) custom-call(bf16[2,256,64]{2,1,0:T(8,128)(2,1)} %get-tuple-element.14.refs_0_, bf16[2,256,64]{2,1,0:T(8,128)(2,1)} %get-tuple-element.15.refs_1_, bf16[256,1024]{1,0:T(8,128)(2,1)} %get-tuple-element.16.refs_2_, ...), custom_call_target="tpu_custom_call" | custom-call | tf_op jit(solution)/shard_map/pallas_call | solution.py:639

commit v3 on v2

--- a/solution.py
+++ b/solution.py
@@ -129,6 +129,8 @@
     for i, name in enumerate(names):
         src = hbm[name].at[gy] if name in BY_GY else hbm[name]
         loads[name] = pltpu.make_async_copy(src, vm[name], in_sem.at[i])
+    early = ("field", "ybd", "gz")
+    for name in early:
         loads[name].start()
 
     barrier = pltpu.get_barrier_semaphore()
@@ -144,9 +146,6 @@
         block = owner % shares * parts + h
         return ref.at[rows, pl.ds(pl.multiple_of(block * width, width), width)]
 
-    def lanes(b):
-        return pl.ds(pl.multiple_of(b * 256, 256), 256)
-
     chips = ngx // 2
     chip, core = gx // 2, gx % 2
     steps = [(c, k) for c in range(1, chips) for k in range(2)] + [(0, 1)]
@@ -161,12 +160,7 @@
 
     rows = KY * rx
 
-    def forward(t, u):
-        for b in range(4):
-            at = slice(b * 256, b * 256 + 256)
-            ybuf[:, at] = dot(vm["ybd"][...], u[:, at]).astype(BF16)
-        if t == 0:
-            loads["gz"].wait()
+    def forward(t):
         for b in range(2):
             cos = dot(ybuf[...], vm["gz"][: NZ * C, b * 256 : b * 256 + 256])
             sin = dot(ybuf[...], vm["gz"][: NZ * C, modes_in + b * 256 : modes_in + b * 256 + 256])
@@ -271,16 +265,18 @@
             pending.append(copy)
         slab(fin.at[t], owner, h)[...] = fs[t, h, g, mine]
 
-    def exchange(t, mix):
+    def exchange(t, mix, beside):
         for h in range(parts):
             send_sums(t, h)
+            if h == 0:
+                beside()
         for h in range(parts):
             send_modes(t, h, mix(h, add_sums(t, h)))
         for h in range(parts):
             for d in range(1, ngy):
                 return_cells(t, h, d, None)
 
-    def backward(t):
+    def backward(t, use):
         per = modes_in // parts
         for h in range(parts):
             got = fin.at[t, pl.ds(0, rows // ngx * (ngx - 1)), pl.ds(h * 2 * per, 2 * per)]
@@ -300,6 +296,7 @@
                 if h == parts - 1:
                     gq[:rows, at] = real.astype(BF16)
                     gq[rows:, at] = imag.astype(BF16)
+                    use(at)
                 else:
                     gacc[:rows, at] = real
                     gacc[rows:, at] = imag
@@ -325,9 +322,16 @@
 
     loads["field"].wait()
     loads["ybd"].wait()
-    forward(0, vm["field"])
+    for b in range(4):
+        at = slice(b * 256, b * 256 + 256)
+        ybuf[:, at] = dot(vm["ybd"][...], vm["field"][:, at]).astype(BF16)
+    loads["gz"].wait()
     for name in names:
-        if name not in ("field", "ybd", "gz"):
+        if name not in early:
+            loads[name].start()
+    forward(0)
+    for name in names:
+        if name not in early:
             loads[name].wait()
 
     bits = kc.bit_length() - 1
@@ -347,14 +351,6 @@
     bc = iota((256, 256), 1) >> 5
     kw[...] = jnp.where(br == bc, wide, 0.0).astype(BF16)
     bias = jnp.concatenate([vm["bias"][...]] * 8, axis=1)
-
-    for b in range(4):
-        at = slice(b * 256, b * 256 + 256)
-        pre[:, at] = dot(vm["field"][:, at], kw[...]) + bias
-
-    for i in range(2 * KX):
-        at = slice(i * C * C, (i + 1) * C * C)
-        wf[:, at] = vm["weight"][:, at].astype(F32)
 
     def weights(h, m):
         k = slice(h * kc, (h + 1) * kc)
@@ -391,6 +387,14 @@
         out = dot(high, ri[...]) + dot(low, ri[...])
         return from_rows(out)
 
+    def widen():
+        for i in range(2 * KX):
+            at = slice(i * C * C, (i + 1) * C * C)
+            wf[:, at] = vm["weight"][:, at].astype(F32)
+        for b in range(4):
+            at = slice(b * 256, b * 256 + 256)
+            pre[:, at] = dot(vm["field"][:, at], kw[...]) + bias
+
     results = []
 
     def give(src, dst):
@@ -398,53 +402,56 @@
         results[-1].start()
 
     give(kw, kw_out)
-    exchange(0, mix_out)
+    exchange(0, mix_out, widen)
     give(vrow, vr_out)
-    backward(0)
-
-    @pl.loop(0, 4)
-    def _(b):
-        v = dot(vm["ybt"][...], gq[:, lanes(b)]) + pre[:, lanes(b)]
+
+    def cell_work(at):
+        v = dot(vm["ybt"][...], gq[:, at]) + pre[:, at]
         root = math.sqrt(2.0 / math.pi)
         square = v * v
-        th = jnp.tanh(root * v * (1.0 + 0.044715 * square))
-        slope = 0.5 * (1.0 + th) + 0.5 * v * (1.0 - th * th) * (
-            root * (1.0 + 3 * 0.044715 * square)
+        th = jnp.tanh(v * (root + (0.044715 * root) * square))
+        slope = 0.5 * (1.0 + th) + v * (1.0 - th * th) * (
+            0.5 * root + (1.5 * 0.044715 * root) * square
         )
-        adj[:, lanes(b)] = (vm["cot"][:, lanes(b)].astype(F32) * slope).astype(BF16)
-
+        value = (vm["cot"][:, at].astype(F32) * slope).astype(BF16)
+        adj[:, at] = value
+        ybuf[:, at] = dot(vm["ybd"][...], value).astype(BF16)
+
+    backward(0, cell_work)
     give(adj, adj_out)
-    forward(1, adj)
-
-    acc[...] = jnp.zeros_like(acc)
-    accb[...] = jnp.zeros_like(accb)
-    ones = jnp.ones((16, rx * ry), BF16)
-
-    @pl.loop(0, 4)
-    def _(b):
-        block = adj[:, lanes(b)]
-        acc[...] += lax.dot_general(
-            vm["field"][:, lanes(b)], block, (((0,), (0,)), ((), ())), preferred_element_type=F32
-        )
-        accb[...] += dot(ones, block)
-
-    pbuf[...] = jnp.zeros_like(pbuf)
-    pbuf[:C, :C] = sum(acc[i * C : (i + 1) * C, i * C : (i + 1) * C] for i in range(8)) * scale
-    pbuf[C:, :C] = sum(accb[:8, i * C : (i + 1) * C] for i in range(8)) * scale
-    for e in range(1, ngx):
-        copy = pltpu.make_async_remote_copy(
-            src_ref=pbuf,
-            dst_ref=precv.at[gx],
-            send_sem=p_send.at[e],
-            recv_sem=p_recv.at[0],
-            device_id={"gx": lax.rem(gx + e, ngx)},
-            device_id_type=MESH,
-        )
-        copy.start()
-        pending.append(copy)
-    precv[gx] = pbuf[...]
-
-    exchange(1, mix_in)
+    forward(1)
+
+    def point_gradients():
+        ones = jnp.ones((16, rx * ry), BF16)
+
+        grad, total = 0.0, 0.0
+        for b in range(4):
+            at = slice(b * 256, b * 256 + 256)
+            block = adj[:, at]
+            grad += lax.dot_general(
+                vm["field"][:, at], block, (((0,), (0,)), ((), ())), preferred_element_type=F32
+            )
+            total += dot(ones, block)
+        acc[...] = grad
+        accb[...] = total
+
+        pbuf[...] = jnp.zeros_like(pbuf)
+        pbuf[:C, :C] = sum(acc[i * C : (i + 1) * C, i * C : (i + 1) * C] for i in range(8)) * scale
+        pbuf[C:, :C] = sum(accb[:8, i * C : (i + 1) * C] for i in range(8)) * scale
+        for e in range(1, ngx):
+            copy = pltpu.make_async_remote_copy(
+                src_ref=pbuf,
+                dst_ref=precv.at[gx],
+                send_sem=p_send.at[e],
+                recv_sem=p_recv.at[0],
+                device_id={"gx": lax.rem(gx + e, ngx)},
+                device_id_type=MESH,
+            )
+            copy.start()
+            pending.append(copy)
+        precv[gx] = pbuf[...]
+
+    exchange(1, mix_in, point_gradients)
     give(hrow, hr_out)
 
     got = precv.at[pl.ds(0, ngx - 1)]
@@ -463,7 +470,7 @@
         pending.append(copy)
     precv2[gy] = pbuf2[...]
 
-    backward(1)
+    backward(1, lambda at: None)
     give(gq, gq_out)
     got = precv2.at[pl.ds(0, ngy - 1)]
     pltpu.make_async_copy(got, got, p_recv.at[1]).wait()

time: 58.8 us -> 58.9 us (level)
  no operation moved by 1% of the time
where the time goes in v3:
time: 58.9 us; the launch traced here: 58.8 us
  Pallas kernels  58.1 us (99%)
  between operations  0.64 us (1%)
    pallas_call x1, Pallas kernels, on_device(): pl.pallas_call(functools.partial(kernel, ngx, ngy, rx, ry, kk, parts, nam...  54.7 us
    pallas_call x1, Pallas kernels, on_device(): pl.pallas_call(functools.partial(finish, scale, kk, parts), out_shape=wan...  3.44 us

profile of v3, /device:TPU:0, one launch (start us, length us, event | category | flops | bytes accessed | tf_op | source)
XLA Modules:
  0.0 58.8 jit_solution(10258378096805689574)
XLA Ops:
  0.6 54.7 %shard_map.120 = (bf16[2,256,64]{2,1,0:T(8,128)(2,1)}, bf16[2,256,64]{2,1,0:T(8,128)(2,1)}, bf16[256,1024]{1,0:T(8,128)(2,1)}, bf16[512,1024]{1,0:T(8,128)(2,1)}...) custom-call(bf16[512,1024]{1,0:T(8,128)(2,1)} %bitcast.5, bf16[4,256,512]{2,1,0:T(8,128)(2,1)} %constant.8.clone.refs_1_, ...), custom_call_target="tpu_custom_call" | custom-call | tf_op jit(solution)/shard_map/pallas_call | solution.py:580
  55.3 3.4 %shard_map.121 = (bf16[512,1024]{1,0:T(8,128)(2,1)}, f32[16,32768]{1,0:T(8,128)}, f32[32,32]{1,0:T(8,128)}, f32[1,32]{1,0:T(1,128)}) custom-call(bf16[2,256,64]{2,1,0:T(8,128)(2,1)} %get-tuple-element.14.refs_0_, bf16[2,256,64]{2,1,0:T(8,128)(2,1)} %get-tuple-element.15.refs_1_, bf16[256,1024]{1,0:T(8,128)(2,1)} %get-tuple-element.16.refs_2_, ...), custom_call_target="tpu_custom_call" | custom-call | tf_op jit(solution)/shard_map/pallas_call | solution.py:646

commit v4 on v3

--- a/solution.py
+++ b/solution.py
@@ -105,11 +105,11 @@
 def kernel(ngx, ngy, rx, ry, kk, parts, names, *refs):
     it = iter(refs)
     hbm = {name: next(it) for name in names}
-    vr_out, hr_out, gq_out, adj_out, kw_out, tot_out = (next(it) for _ in range(6))
+    gs_out, gq_out, adj_out, kw_out, tot_out = (next(it) for _ in range(5))
     vm = {name: next(it) for name in names}
     (ybuf, zout, recv1, send2, recv2, zs, recvs, fs, fin, gq, vexp, hexp, red, prod,
-     adj, vrow, hrow, acc, accb, kw, pbuf, precv, pbuf2, precv2, f2, pre, gacc, tot, wf,
-     perm, permt, ei, eo, ro, ri) = (next(it) for _ in range(35))
+     adj, vrow, hrow, acc, accb, kw, pbuf, precv, pbuf2, precv2, f2, pre, gacc, tot, wf, gs,
+     perm, permt, ei, eo, ro, ri) = (next(it) for _ in range(36))
     (in_sem, out_sem, s1_send, s1_recv, s2_send, s2_recv, g_send, g_recv, f_send, f_recv,
      p_send, p_recv) = (next(it) for _ in range(12))
 
@@ -391,9 +391,6 @@
         for i in range(2 * KX):
             at = slice(i * C * C, (i + 1) * C * C)
             wf[:, at] = vm["weight"][:, at].astype(F32)
-        for b in range(4):
-            at = slice(b * 256, b * 256 + 256)
-            pre[:, at] = dot(vm["field"][:, at], kw[...]) + bias
 
     results = []
 
@@ -403,7 +400,6 @@
 
     give(kw, kw_out)
     exchange(0, mix_out, widen)
-    give(vrow, vr_out)
 
     def cell_work(at):
         v = dot(vm["ybt"][...], gq[:, at]) + pre[:, at]
@@ -417,6 +413,9 @@
         adj[:, at] = value
         ybuf[:, at] = dot(vm["ybd"][...], value).astype(BF16)
 
+    for b in range(4):
+        at = slice(b * 256, b * 256 + 256)
+        pre[:, at] = dot(vm["field"][:, at], kw[...]) + bias
     backward(0, cell_work)
     give(adj, adj_out)
     forward(1)
@@ -452,7 +451,6 @@
         precv[gx] = pbuf[...]
 
     exchange(1, mix_in, point_gradients)
-    give(hrow, hr_out)
 
     got = precv.at[pl.ds(0, ngx - 1)]
     pltpu.make_async_copy(got, got, p_recv.at[0]).wait()
@@ -470,6 +468,16 @@
         pending.append(copy)
     precv2[gy] = pbuf2[...]
 
+    for h in range(parts):
+        k = slice(h * kc, (h + 1) * kc)
+        vexp[...] = dot(vrow[h], ei[...])
+        hexp[...] = dot(hrow[h], eo[...])
+        for m in range(KX):
+            a, b = pair(m)
+            vr, vi, hr, hi = vexp[a], vexp[b], hexp[a] * scale, hexp[b] * scale
+            gs[k, m * 2048 : m * 2048 + 1024] = vr * hr + vi * hi
+            gs[k, m * 2048 + 1024 : m * 2048 + 2048] = vr * hi - vi * hr
+    give(gs, gs_out)
     backward(1, lambda at: None)
     give(gq, gq_out)
     got = precv2.at[pl.ds(0, ngy - 1)]
@@ -482,50 +490,26 @@
         copy.wait_send()
 
 
-def finish(scale, kk, parts, *refs):
-    (vr_in, hr_in, gq_in, adj_in, kw_in, tot_in, ybt_in, gf_out, gs_out, gp_out, gb_out,
-     vrow, hrow, gq, adj, kw, tot, ybt, gf, gs, gp, gb, vexp, hexp, ei, eo, in_sem,
-     out_sem) = refs
-    kc = kk // parts
-    n = KX * kc
-    loads = [
-        pltpu.make_async_copy(src, dst, in_sem.at[i])
-        for i, (src, dst) in enumerate(
-            [(vr_in, vrow), (hr_in, hrow), (gq_in, gq), (adj_in, adj), (kw_in, kw),
-             (tot_in, tot), (ybt_in.at[lax.axis_index("gy")], ybt)]
-        )
-    ]
+def finish(*refs):
+    (gs_in, gq_in, adj_in, kw_in, tot_in, ybt_in, gf_out, gs_out, gp_out, gb_out,
+     gs, gq, adj, kw, tot, ybt, gf, gp, gb, in_sem, out_sem) = refs
+    cuts = 4
+    lanes = gs.shape[1] // cuts
+    pieces = [pl.ds(i * lanes, lanes) for i in range(cuts)]
+    pairs = [(gq_in, gq), (adj_in, adj), (kw_in, kw), (ybt_in.at[lax.axis_index("gy")], ybt),
+             (tot_in, tot)]
+    pairs += [(gs_in.at[:, at], gs.at[:, at]) for at in pieces]
+    loads = [pltpu.make_async_copy(a, b, in_sem.at[i]) for i, (a, b) in enumerate(pairs)]
     for load in loads:
         load.start()
-    fill(ei, over_out)
-    fill(eo, over_in)
     results = []
 
     def give(src, dst):
         results.append(pltpu.make_async_copy(src, dst, out_sem.at[len(results)]))
         results[-1].start()
 
-    loads[0].wait()
-    loads[1].wait()
-    for h in range(parts):
-        k = slice(h * kc, (h + 1) * kc)
-        vexp[...] = dot(vrow[h], ei[...])
-        hexp[...] = dot(hrow[h], eo[...])
-        for m in range(KX):
-            a, b = slice(m * kc, (m + 1) * kc), slice(n + m * kc, n + (m + 1) * kc)
-            vr, vi, hr, hi = vexp[a], vexp[b], hexp[a] * scale, hexp[b] * scale
-            gs[k, m * 2048 : m * 2048 + 1024] = vr * hr + vi * hi
-            gs[k, m * 2048 + 1024 : m * 2048 + 2048] = vr * hi - vi * hr
-        if parts == 1:
-            give(gs, gs_out)
-        else:
-            give(gs.at[pl.ds(h * kc, kc)], gs_out.at[pl.ds(h * kc, kc)])
-    for load in loads[2:]:
+    for load in loads[:4]:
         load.wait()
-    gp[...] = tot[:C, :C]
-    gb[...] = tot[C : C + 1, :C]
-    give(gp, gp_out)
-    give(gb, gb_out)
     for b in range(4):
         at = pl.ds(b * 256, 256)
         back = lax.dot_general(
@@ -533,6 +517,13 @@
         )
         gf[:, at] = (dot(ybt[...], gq[:, at]) + back).astype(BF16)
         give(gf.at[:, at], gf_out.at[:, at])
+        loads[5 + b].wait()
+        give(gs.at[:, pieces[b]], gs_out.at[:, pieces[b]])
+    loads[4].wait()
+    gp[...] = tot[:C, :C]
+    gb[...] = tot[C : C + 1, :C]
+    give(gp, gp_out)
+    give(gb, gb_out)
     for copy in results:
         copy.wait()
 
@@ -564,10 +555,8 @@
     n2 = PM * kc
     hbm = pl.BlockSpec(memory_space=pltpu.HBM)
     dma = pltpu.SemaphoreType.DMA
-    rows_type = jax.ShapeDtypeStruct((parts, n2, 2 * C), BF16)
     between = (
-        rows_type,
-        rows_type,
+        jax.ShapeDtypeStruct(spectral_weight.shape, F32),
         jax.ShapeDtypeStruct((2 * rows, depth), BF16),
         jax.ShapeDtypeStruct((cells, depth), BF16),
         jax.ShapeDtypeStruct((256, 256), BF16),
@@ -613,6 +602,7 @@
             pltpu.VMEM((2 * rows, depth), F32),
             pltpu.VMEM((C + 8, 128), F32),
             pltpu.VMEM(spectral_weight.shape, F32),
+            pltpu.VMEM(spectral_weight.shape, F32),
             pltpu.VMEM((n2, n2), BF16),
             pltpu.VMEM((n2, n2), BF16),
             pltpu.VMEM((2 * C, C * C), BF16),
@@ -642,23 +632,15 @@
         jax.ShapeDtypeStruct((C, C), F32),
         jax.ShapeDtypeStruct((1, C), F32),
     )
-    scale = 1.0 / math.sqrt(nx * ngy * ry * NZ)
     grad_field, grad_spectral, grad_point, grad_bias = pl.pallas_call(
-        functools.partial(finish, scale, kk, parts),
+        finish,
         out_shape=wanted,
         in_specs=[hbm] * (len(between) + 1),
         out_specs=(hbm,) * len(wanted),
         scratch_shapes=room(between)
         + [pltpu.VMEM(consts["ybt"].shape[1:], BF16)]
-        + room(wanted)
-        + [
-            pltpu.VMEM((n2, C * C), F32),
-            pltpu.VMEM((n2, C * C), F32),
-            pltpu.VMEM((2 * C, C * C), BF16),
-            pltpu.VMEM((2 * C, C * C), BF16),
-            dma((len(between) + 1,)),
-            dma((parts + 6,)),
-        ],
+        + room(wanted[:1] + wanted[2:])
+        + [dma((len(between) + 5,)), dma((10,))],
         compiler_params=pltpu.CompilerParams(vmem_limit_bytes=VMEM_LIMIT),
     )(*kept, consts["ybt"])
     return (

time: 58.9 us -> 59.8 us (1.015)
  Pallas kernels: 58.1 us -> 59 us
    pallas_call x1, Pallas kernels: 3.44 us -> 4.35 us  [on_device(): pl.pallas_call(finish, out_shape=wanted, in_specs=[hbm] * (len(between) +...]
where the time goes in v4:
time: 59.8 us; the launch traced here: 59.7 us
  Pallas kernels  59 us (99%)
  between operations  0.64 us (1%)
    pallas_call x1, Pallas kernels, on_device(): pl.pallas_call(functools.partial(kernel, ngx, ngy, rx, ry, kk, parts, nam...  54.7 us
    pallas_call x1, Pallas kernels, on_device(): pl.pallas_call(finish, out_shape=wanted, in_specs=[hbm] * (len(between) +...  4.35 us

profile of v4, /device:TPU:0, one launch (start us, length us, event | category | flops | bytes accessed | tf_op | source)
XLA Modules:
  0.0 59.7 jit_solution(18393620204041131546)
XLA Ops:
  0.6 54.7 %shard_map.120 = (f32[16,32768]{1,0:T(8,128)}, bf16[256,1024]{1,0:T(8,128)(2,1)}, bf16[512,1024]{1,0:T(8,128)(2,1)}, bf16[256,256]{1,0:T(8,128)(2,1)}, f32[40,128]{1,0:T(8,128)}) custom-call(bf16[512,1024]{1,0:T(8,128)(2,1)} %bitcast.5, bf16[4,256,512]{2,1,0:T(8,128)(2,1)} %constant.8.clone.refs_1_, bf16[1120,1024]{1,0:T(8,128)(2,1)} %constant.9.clone.refs_2_, ...), custom_call_target="tpu_custom_call" | custom-call | tf_op jit(solution)/shard_map/pallas_call | solution.py:569
  55.3 4.3 %shard_map.121 = (bf16[512,1024]{1,0:T(8,128)(2,1)}, f32[16,32768]{1,0:T(8,128)}, f32[32,32]{1,0:T(8,128)}, f32[1,32]{1,0:T(1,128)}) custom-call(f32[16,32768]{1,0:T(8,128)} %get-tuple-element.13.refs_0_, bf16[256,1024]{1,0:T(8,128)(2,1)} %get-tuple-element.14.refs_1_, bf16[512,1024]{1,0:T(8,128)(2,1)} %get-tuple-element.15.refs_2_, ...), custom_call_target="tpu_custom_call" | custom-call | tf_op jit(solution)/shard_map/pallas_call | solution.py:635
